TPU v7x, 512 devices: a whole 4x4x16 slice. The times are simulated.
512 devices in a mesh: rows: 64 (over z, y), cols: 8 (over x, core).
Axes of the slice: x: 4, y: 4, z: 16, core: 2. Of those that a mesh axis runs over, the one named last changes fastest.
Arguments:
- tiles: float32 [12288, 128, 128], P(('rows', 'cols')), may hold values from -0.5 to 0.5
- tile_row: int32 [12288], P(('rows', 'cols')), may hold values from 0 to 255
- tile_col: int32 [12288], P(('rows', 'cols')), may hold values from 0 to 1023
- tile_counts: int32 [512], P(('rows', 'cols')), may hold values from 1 to 24, as said below
- scores: float32 [16384, 128], P('rows'), may hold values from -40 to 40
Outputs:
- weights_fit: float32 [8192, 128], P(('cols', 'rows'))
- residual: float32 [16384, 128], P('rows')
Inputs may be any that keep to these rules, and one draw needn't show every extreme that they name: `tile_counts`: every device has at least one live slot, and at least one device has all 24 slots live.
All inputs are finite; a program needn't handle non-finite values.
Results may differ from a plain program's by a relative error of at most 0.0015.
Values sent between devices are 32-bit elements; how exact they have to be, the bound alone decides.
No kernel may reach another device: no remote copies, remote signals or barrier semaphores. Data moves between devices by JAX's collectives and lax.ppermute only.
A program may use at most 64 MiB of HBM per device.

v0:
```python
import jax
import jax.numpy as jnp
from jax import lax
from jax.sharding import PartitionSpec as P

COLBLOCKS = 8192
ITERS = 3


group_size = 8


def local(tiles, tile_row, tile_col, tile_counts, scores):
    highest = lax.Precision.HIGHEST
    capacity = tiles.shape[0]
    tile_edge = tiles.shape[1]
    row_blocks = scores.shape[0]
    rows_count = lax.axis_size("rows")
    cols_count = lax.axis_size("cols")
    col_blocks = COLBLOCKS // cols_count
    share_blocks = col_blocks // rows_count
    row_share = row_blocks // cols_count
    rows_place = lax.axis_index("rows")
    cols_place = lax.axis_index("cols")
    live_count = tile_counts[0]
    group_turns = (live_count + group_size - 1) // group_size
    live = (jnp.arange(capacity, dtype=jnp.int32) < live_count).astype(jnp.float32)
    row_hits = (tile_row[None, :] == jnp.arange(row_blocks, dtype=jnp.int32)[:, None]).astype(
        jnp.float32
    ) * live[None, :]
    col_hits = (tile_col[None, :] == jnp.arange(col_blocks, dtype=jnp.int32)[:, None]).astype(
        jnp.float32
    ) * live[None, :]

    def backward_partial(vector):

        def backward_add_group(turn, total):
            start = turn * group_size
            block = lax.dynamic_slice_in_dim(tiles, start, group_size, 0)
            picked = vector[lax.dynamic_slice_in_dim(tile_row, start, group_size, 0)]
            images = jnp.einsum("tij,ti->tj", block, picked, precision=highest)
            hits = lax.dynamic_slice_in_dim(col_hits, start, group_size, 1)
            return total + jnp.dot(hits, images, precision=highest)

        return lax.fori_loop(
            0, group_turns, backward_add_group, jnp.zeros((col_blocks, tile_edge), jnp.float32)
        )

    def gradient_of(vector):
        return lax.psum(backward_partial(vector), "rows")

    def own_share(vector):
        return lax.dynamic_slice_in_dim(vector, rows_place * share_blocks, share_blocks, 0)

    def norm_of(gradient):
        piece = own_share(gradient)
        return lax.psum(jnp.sum(piece * piece), ("rows", "cols"))

    residual = scores
    gradient = gradient_of(residual)
    weights_fit = jnp.zeros(gradient.shape, jnp.float32)
    norm_now = norm_of(gradient)
    direction = gradient
    for iteration in range(ITERS):
        forward_vector = direction

        def forward_add_group(turn, total):
            start = turn * group_size
            block = lax.dynamic_slice_in_dim(tiles, start, group_size, 0)
            picked = forward_vector[lax.dynamic_slice_in_dim(tile_col, start, group_size, 0)]
            images = jnp.einsum("tij,tj->ti", block, picked, precision=highest)
            hits = lax.dynamic_slice_in_dim(row_hits, start, group_size, 1)
            return total + jnp.dot(hits, images, precision=highest)

        partial_sum = lax.fori_loop(
            0, group_turns, forward_add_group, jnp.zeros((row_blocks, tile_edge), jnp.float32)
        )
        image = lax.psum(partial_sum, "cols")
        image_piece = lax.dynamic_slice_in_dim(image, cols_place * row_share, row_share, 0)
        step_size = norm_now / lax.psum(jnp.sum(image_piece * image_piece), ("rows", "cols"))
        weights_fit = weights_fit + step_size * direction
        residual = residual - step_size * image
        if iteration + 1 < ITERS:
            gradient = gradient_of(residual)
            norm_next = norm_of(gradient)
            direction = gradient + norm_next / norm_now * direction
            norm_now = norm_next
    return (own_share(weights_fit), residual)


def solution(mesh):
    return jax.shard_map(
        local,
        mesh=mesh,
        in_specs=(
            P(("rows", "cols"), None, None),
            P(("rows", "cols")),
            P(("rows", "cols")),
            P(("rows", "cols")),
            P("rows", None),
        ),
        out_specs=(P(("cols", "rows"), None), P("rows", None)),
        check_vma=False,
    )
```

profile of v0, /device:TPU:1, one launch (start us, length us, event | category | flops | bytes accessed | tf_op | source)
XLA Modules:
  0.0 1604.6 jit_solution(15781941050646454876)
XLA Ops:
  7.9 0.7 fusion.30
  8.7 4.9 while.60
  8.7 0.7 compare_select_fusion.12
  9.5 1.5 gather_fusion
  10.9 1.6 fusion.80
  12.5 1.0 convolution_add_fusion.12
  13.6 0.8 copy-done.1
  14.5 0.7 fusion.31
  15.2 269.9 %all-reduce.8.cloned.1.call-done = f32[1024,128]{1,0:T(8,128)} async-done(((f32[1024,128]{1,0:T(8,128)}), f32[1024,128]{1,0:T(8,128)}) %all-reduce.8.cloned.1.call-update) | async-done | bytes 524304 | tf_op jit(solution)/shard_map/psum | solution.py:50
  285.1 4.1 while.61
  285.2 1.6 gather_fusion.1
  286.8 2.0 fusion.85
  289.2 0.6 copy-done.5
  290.0 1.4 multiply_reduce_fusion.5
  291.4 83.9 %all-reduce.10.cloned.1.call-done = f32[256,128]{1,0:T(8,128)} async-done(((f32[256,128]{1,0:T(8,128)}), f32[256,128]{1,0:T(8,128)}) %all-reduce.10.cloned.1.call-update) | async-done | bytes 131088 | tf_op jit(solution)/shard_map/psum | solution.py:78
  375.3 1.3 multiply_reduce_fusion.2
  376.6 105.9 %all-reduce = (f32[]{:T(128)}, f32[]{:T(128)}) all-reduce(f32[]{:T(128)} %multiply_reduce_fusion.5, f32[]{:T(128)} %multiply_reduce_fusion.2), channel_id=1, replica_groups=mesh['rows'=64,'cols'=8] {'rows','cols'}, use_global_device_ids=true, to_apply=%region_4.5 | all-reduce | flops 2 | bytes 16 | tf_op jit(solution)/shard_map/psum | solution.py:57
  483.8 0.9 multiply_subtract_fusion.2
  484.8 3.3 while.62
  485.5 1.6 fusion.90
  487.1 1.0 convolution_add_fusion.14
  488.1 0.8 copy-done.2
  489.0 256.8 %all-reduce.12.cloned.1.call-done = f32[1024,128]{1,0:T(8,128)} async-done(((f32[1024,128]{1,0:T(8,128)}), f32[1024,128]{1,0:T(8,128)}) %all-reduce.12.cloned.1.call-update) | async-done | bytes 524304 | tf_op jit(solution)/shard_map/psum | solution.py:50
  745.8 1.3 multiply_reduce_fusion.4
  747.2 109.7 %psum.89 = f32[]{:T(128)} all-reduce(f32[]{:T(128)} %multiply_reduce_fusion.4), channel_id=1, replica_groups=mesh['rows'=64,'cols'=8] {'rows','cols'}, use_global_device_ids=true, to_apply=%region_14.15 | all-reduce | flops 1 | bytes 8 | tf_op jit(solution)/shard_map/psum | solution.py:57
  858.2 1.1 multiply_add_fusion.1
  859.4 2.0 while.63
  860.1 0.9 fusion.95
  861.4 0.6 copy-done.6
  862.2 70.7 %all-reduce.14.cloned.1.call-done = f32[256,128]{1,0:T(8,128)} async-done(((f32[256,128]{1,0:T(8,128)}), f32[256,128]{1,0:T(8,128)}) %all-reduce.14.cloned.1.call-update) | async-done | bytes 131088 | tf_op jit(solution)/shard_map/psum | solution.py:78
  932.9 1.3 multiply_reduce_fusion.1
  934.2 105.8 %psum.91 = f32[]{:T(128)} all-reduce(f32[]{:T(128)} %multiply_reduce_fusion.1), channel_id=1, replica_groups=mesh['rows'=64,'cols'=8] {'rows','cols'}, use_global_device_ids=true, to_apply=%region_19.20 | all-reduce | flops 1 | bytes 8 | tf_op jit(solution)/shard_map/psum | solution.py:80
  1041.4 0.9 multiply_subtract_fusion.1
  1042.4 2.3 while.64
  1043.6 1.0 convolution_add_fusion.16
  1044.7 0.8 copy-done.3
  1045.5 254.8 %all-reduce.16.cloned.1.call-done = f32[1024,128]{1,0:T(8,128)} async-done(((f32[1024,128]{1,0:T(8,128)}), f32[1024,128]{1,0:T(8,128)}) %all-reduce.16.cloned.1.call-update) | async-done | bytes 524304 | tf_op jit(solution)/shard_map/psum | solution.py:50
  1300.4 1.3 multiply_reduce_fusion.3
  1301.7 109.7 %psum.93 = f32[]{:T(128)} all-reduce(f32[]{:T(128)} %multiply_reduce_fusion.3), channel_id=1, replica_groups=mesh['rows'=64,'cols'=8] {'rows','cols'}, use_global_device_ids=true, to_apply=%region_24.25 | all-reduce | flops 1 | bytes 8 | tf_op jit(solution)/shard_map/psum | solution.py:57
  1412.7 1.1 multiply_add_fusion
  1413.8 2.0 while.65
  1414.5 0.9 fusion.105
  1415.9 0.6 copy-done.4
  1416.5 70.7 %all-reduce.18.cloned.1.call-done = f32[256,128]{1,0:T(8,128)} async-done(((f32[256,128]{1,0:T(8,128)}), f32[256,128]{1,0:T(8,128)}) %all-reduce.18.cloned.1.call-update) | async-done | bytes 131088 | tf_op jit(solution)/shard_map/psum | solution.py:78
  1487.2 1.3 multiply_reduce_fusion
  1488.6 105.8 %psum.95 = f32[]{:T(128)} all-reduce(f32[]{:T(128)} %multiply_reduce_fusion), channel_id=1, replica_groups=mesh['rows'=64,'cols'=8] {'rows','cols'}, use_global_device_ids=true, to_apply=%region_29.30 | all-reduce | flops 1 | bytes 8 | tf_op jit(solution)/shard_map/psum | solution.py:80
  1595.6 1.6 multiply_subtract_fusion
  1597.2 0.6 fusion.32
  (54 shorter events, 5.0 us)
Async XLA Ops:
  7.2 277.9 %all-reduce.8.cloned.1.call-start = ((), (), s32[]{:S(2)}) async-start(), calls=%async_computation | async-start | bytes 1048576 | tf_op jit(solution)/shard_map/psum | solution.py:50
  8.7 276.4 %copy-start.9 = (s32[24]{0:T(128)S(1)}, s32[24]{0:T(128)}, u32[]{:S(2)}) copy-start(s32[24]{0:T(128)} %param.19) | copy-start | bytes 292
  13.6 0.8 copy-start.1
  14.4 360.8 %all-reduce.10.cloned.1.call-start = ((), (), s32[]{:S(2)}) async-start(), calls=%async_computation.1 | async-start | bytes 262144 | tf_op jit(solution)/shard_map/psum | solution.py:78
  285.1 198.7 %copy-start.8 = (f32[256,128]{1,0:T(8,128)S(1)}, f32[256,128]{1,0:T(8,128)}, u32[]{:S(2)}) copy-start(f32[256,128]{1,0:T(8,128)} %get-tuple-element.817) | copy-start | bytes 393220
  285.1 199.7 %copy-start.10 = (s32[24]{0:T(128)S(1)}, s32[24]{0:T(128)}, u32[]{:S(2)}) copy-start(s32[24]{0:T(128)} %get-tuple-element.825) | copy-start | bytes 292
  289.2 0.7 copy-start.5
  289.9 455.9 %all-reduce.12.cloned.1.call-start = ((), (), s32[]{:S(2)}) async-start(), calls=%async_computation.2 | async-start | bytes 1048576 | tf_op jit(solution)/shard_map/psum | solution.py:50
  484.8 373.5 %copy-start.7 = (f32[1024,128]{1,0:T(8,128)S(1)}, f32[1024,128]{1,0:T(8,128)}, u32[]{:S(2)}) copy-start(f32[1024,128]{1,0:T(8,128)} %get-tuple-element.813) | copy-start | bytes 1572868
  488.1 0.8 copy-start.2
  488.1 371.3 %copy-start = (f32[24,128,128]{2,1,0:T(8,128)S(1)}, f32[24,128,128]{2,1,0:T(8,128)}, u32[]{:S(2)}) copy-start(f32[24,128,128]{2,1,0:T(8,128)} %get-tuple-element.792) | copy-start | bytes 4718596
  489.0 443.9 %all-reduce.14.cloned.1.call-start = ((), (), s32[]{:S(2)}) async-start(), calls=%async_computation.3 | async-start | bytes 262144 | tf_op jit(solution)/shard_map/psum | solution.py:78
  861.4 0.7 copy-start.6
  862.1 438.3 %all-reduce.16.cloned.1.call-start = ((), (), s32[]{:S(2)}) async-start(), calls=%async_computation.4 | async-start | bytes 1048576 | tf_op jit(solution)/shard_map/psum | solution.py:50
  1044.6 0.8 copy-start.3
  1045.5 441.8 %all-reduce.18.cloned.1.call-start = ((), (), s32[]{:S(2)}) async-start(), calls=%async_computation.5 | async-start | bytes 262144 | tf_op jit(solution)/shard_map/psum | solution.py:78
  1415.8 0.7 copy-start.4
Sparse Core Ops, SparseCore 0:
  14.5 270.4 all-reduce.7
  290.0 85.1 all-reduce.9
  489.1 256.7 all-reduce.11
  862.2 70.6 all-reduce.13
  1045.6 254.7 all-reduce.15
  1416.6 70.5 all-reduce.17
where the time goes:
time: 1610 us; the launch traced here: 1600 us
  waiting for transfers between devices  1010 us (63%)
  blocking collectives  537 us (33%)
  between operations  21.7 us (1%)
  other arithmetic  16.9 us (1%)
    psum x3, waiting for transfers between devices, gradient_of(): return lax.psum(backward_partial(vector), 'rows')  782 us
    psum x3, blocking collectives, norm_of(): return lax.psum(jnp.sum(piece * piece), ('rows', 'cols'))  325 us
    psum x3, waiting for transfers between devices, local(): image = lax.psum(partial_sum, 'cols')  225 us
    psum x2, blocking collectives, local(): lax.psum(jnp.sum(image_piece * image_piece), ('rows', 'cols'))  212 us
  transfers between devices with their start and end apart: 6, of which 6 were waited for; matrix products, arithmetic and copies ran while one was open for 0% of the time, Pallas kernels for 0%

commit v1 on v0

v1 whole, which is shorter than its diff:
```python
import functools

import jax
import jax.numpy as jnp
from jax import lax
from jax.experimental import pallas as pl
from jax.experimental.pallas import tpu as pltpu
from jax.sharding import Mesh, PartitionSpec as P


Z, Y, X, CORE = 16, 4, 4, 2
COLS = X * CORE
ROWS = Z * Y
CAP = 24
TB = 128
ROW_BLOCKS = 256
SHARE = 16
WANT = CAP + SHARE
LINE = Z * CAP
EXTRA = 8
MSG = CAP + EXTRA
HAND = WANT + EXTRA
F32 = jnp.float32
BF16 = jnp.bfloat16


def iota(shape, dim):
    return lax.broadcasted_iota(jnp.int32, shape, dim)


def two_parts(x):
    high = x.astype(BF16).astype(F32)
    return high, x - high


def side_by_side(x):
    high, low = two_parts(x)
    return jnp.concatenate([high, low], axis=1).astype(BF16)


def picked_sum(hits, values):
    out = jnp.dot(hits, side_by_side(values), preferred_element_type=F32)
    return out[:, :TB] + out[:, TB:]


def times_tiles(vectors, split_ref, live, transposed):
    sub = iota((8, TB), 0)
    groups = []
    for g in range(CAP // 8):
        high, low = two_parts(vectors[8 * g : 8 * g + 8])
        both = jnp.concatenate([high, low], axis=0).astype(BF16)
        if transposed:
            both = jnp.concatenate([both, both], axis=1)
        total = jnp.zeros((8, TB), F32)
        for k in range(8):
            tile = split_ref[8 * g + k]
            if transposed:
                out = jnp.dot(both, tile, preferred_element_type=F32)
            else:
                out = lax.dot_general(
                    both, tile, (((1,), (1,)), ((), ())), preferred_element_type=F32
                )
                out = out[:, :TB] + out[:, TB:]
            total = jnp.where(sub == k, out[:8] + out[8:], total)
        groups.append(jnp.where(sub + 8 * g < live, total, 0.0))
    return jnp.concatenate(groups, axis=0)


def pick_rows(source, row_ref, picked):
    for j in range(CAP):
        picked[j : j + 1, :] = source[pl.ds(row_ref[j], 1), :]


def hits_of(wanted, lane_rows, width):
    pieces = [
        jnp.where(wanted == lane_rows[i : i + 1, :], 1.0, 0.0) for i in range(lane_rows.shape[0])
    ]
    return jnp.concatenate(pieces, axis=1)[:, :width].astype(BF16)


def index_rows(index_ref, live, base):
    flat = iota((EXTRA, TB), 0) * TB + iota((EXTRA, TB), 1)
    rows = jnp.zeros((EXTRA, TB), F32)
    for j in range(CAP):
        value = jnp.where(j < live, index_ref[j] + 1, 0).astype(F32)
        rows = jnp.where(flat == base + j, value, rows)
    return rows


def lane_sum(x):
    return jnp.sum(x, axis=0, keepdims=True)


def total_of(row):
    return jnp.sum(row, axis=1, keepdims=True)


def stack_rows(rows):
    sub = iota((EXTRA, TB), 0)
    out = jnp.zeros((EXTRA, TB), F32)
    for k, row in enumerate(rows):
        out = jnp.where(sub == k, row, out)
    return out


def first_kernel(row_ref, col_ref, live_ref, tiles_ref, scores_ref, out_ref, split_ref, picked):
    live = live_ref[0]
    for j in range(CAP):
        high, low = two_parts(tiles_ref[j])
        split_ref[j, :TB, :] = high.astype(BF16)
        split_ref[j, TB:, :] = low.astype(BF16)
    pick_rows(scores_ref, row_ref, picked)
    sums = times_tiles(picked[...], split_ref, live, True)
    extra = index_rows(col_ref, live, lax.axis_index("z") * CAP)
    for i in range(Z):
        out_ref[i, :CAP, :] = sums
        out_ref[i, CAP:, :] = extra


def relay_kernel(in_ref, out_ref):
    extra = in_ref[0, CAP:, :]
    for i in range(1, Z):
        extra = extra + in_ref[i, CAP:, :]
    for y in range(Y):
        for i in range(Z):
            out_ref[y, CAP * i : CAP * (i + 1), :] = in_ref[i, :CAP, :]
        out_ref[y, LINE:, :] = extra


def send_forward(vectors, split_ref, live, extra, out_ref):
    sums = times_tiles(vectors, split_ref, live, False)
    for i in range(COLS):
        out_ref[i, :CAP, :] = sums
        out_ref[i, CAP:, :] = extra


def gathered_kernel(row_ref, live_ref, in_ref, split_ref, out_ref, gradient_ref, hits_ref):
    live = live_ref[0]
    z, y = lax.axis_index("z"), lax.axis_index("y")
    lines = LINE // TB
    index = [in_ref[i, LINE : LINE + lines, :] for i in range(Y)]
    own_rows = jnp.zeros((lines, TB), F32)
    for i in range(Y):
        own_rows = jnp.where(y == i, index[i], own_rows)
    own_wanted = jnp.zeros((WANT, 1), F32)
    lane, sub = iota((CAP, TB), 1), iota((CAP, TB), 0)
    for i in range(Y):
        found = jnp.zeros((CAP, TB), F32)
        for k in range(lines):
            found = jnp.where(lane + k * TB == sub + z * CAP, index[i][k : k + 1, :], found)
        tile_part = jnp.sum(found, axis=1, keepdims=True)
        share_part = ((z * Y + i) * SHARE + 1 + iota((SHARE, 1), 0)).astype(F32)
        wanted = jnp.concatenate([tile_part, share_part], axis=0)
        hits_ref[WANT * i : WANT * (i + 1), :] = hits_of(wanted, own_rows, LINE)
        own_wanted = jnp.where(y == i, wanted, own_wanted)
    gradient = jnp.zeros((WANT, TB), F32)
    for i in range(Y):
        gradient += picked_sum(hits_of(own_wanted, index[i], LINE), in_ref[i, :LINE, :])
    gradient_ref[...] = gradient
    place = lax.axis_index("x") * CORE + lax.axis_index("core")
    extra = index_rows(row_ref, live, place * MSG)
    send_forward(gradient[:CAP], split_ref, live, extra, out_ref)


def send_backward(image_ref, row_ref, split_ref, live, scalars, out_ref, picked):
    pick_rows(image_ref, row_ref, picked)
    sums = times_tiles(picked[...], split_ref, live, True)
    extra = stack_rows(scalars)
    for i in range(Z):
        out_ref[i, :CAP, :] = sums
        out_ref[i, CAP:, :] = extra


def first_image_kernel(
    row_ref, live_ref, in_ref, split_ref, scores_ref, out_ref, image_ref, hits_ref, picked
):
    extra = in_ref[0, CAP:, :]
    for i in range(1, COLS):
        extra = extra + in_ref[i, CAP:, :]
    wanted = (iota((ROW_BLOCKS, 1), 0) + 1).astype(F32)
    hits = hits_of(wanted, extra[: COLS * MSG // TB], COLS * MSG)
    hits_ref[...] = hits
    image = picked_sum(hits, in_ref[...].reshape(COLS * MSG, TB))
    image_ref[...] = image
    scalars = [lane_sum(image * scores_ref[...]), lane_sum(image * image)]
    send_backward(image_ref, row_ref, split_ref, live_ref[0], scalars, out_ref, picked)


def hand_kernel(in_ref, hits_ref, out_ref):
    extra = in_ref[0, CAP:, :]
    for i in range(1, Z):
        extra = extra + in_ref[i, CAP:, :]
    sums = picked_sum(hits_ref[...], in_ref[:, :CAP, :].reshape(LINE, TB))
    for i in range(Y):
        out_ref[i, :WANT, :] = sums[WANT * i : WANT * (i + 1)]
        out_ref[i, WANT:, :] = extra


def added(in_ref):
    total = in_ref[0]
    for i in range(1, in_ref.shape[0]):
        total = total + in_ref[i]
    return total


def second_gradient_kernel(
    live_ref, in_ref, split_ref, gradient_ref, out_ref, product_ref, next_ref, state_ref
):
    total = added(in_ref)
    product = total[:WANT]
    norm = total_of(total[WANT : WANT + 1])
    image_norm = total_of(total[WANT + 1 : WANT + 2])
    step = norm / image_norm
    following = gradient_ref[...] - step * product
    product_ref[...] = product
    next_ref[...] = following
    state_ref[...] = stack_rows([norm, image_norm, step])
    send_forward(
        following[:CAP], split_ref, live_ref[0], jnp.zeros((EXTRA, TB), F32), out_ref
    )


def second_image_kernel(
    row_ref, live_ref, in_ref, split_ref, hits_ref, scores_ref, old_ref, state_ref,
    out_ref, image_ref, picked,
):
    image = picked_sum(hits_ref[...], in_ref[...].reshape(COLS * MSG, TB))
    image_ref[...] = image
    old = old_ref[...]
    residual = scores_ref[...] - state_ref[2:3, :] * old
    scalars = [lane_sum(image * residual), lane_sum(image * image), lane_sum(image * old)]
    send_backward(image_ref, row_ref, split_ref, live_ref[0], scalars, out_ref, picked)


def third_gradient_kernel(
    live_ref, in_ref, split_ref, first_ref, second_ref, product_ref, state_ref,
    out_ref, keep_ref, later_ref,
):
    total = added(in_ref)
    old_norm, old_image_norm, old_step = state_ref[0:1, :], state_ref[1:2, :], state_ref[2:3, :]
    norm = total_of(total[WANT : WANT + 1])
    ratio = norm / old_norm
    image_norm = (
        total_of(total[WANT + 1 : WANT + 2])
        + 2.0 * ratio * total_of(total[WANT + 2 : WANT + 3])
        + ratio * ratio * old_image_norm
    )
    step = norm / image_norm
    first, second = first_ref[...], second_ref[...]
    product = total[:WANT] + ratio * product_ref[...]
    third = second - step * product
    direction = second + ratio * first
    weights = old_step * first + step * direction
    keep_ref[0] = third[CAP:]
    keep_ref[1] = direction[CAP:]
    keep_ref[2] = weights[CAP:]
    later_ref[...] = stack_rows([norm, image_norm, step, ratio])
    send_forward(third[:CAP], split_ref, live_ref[0], jnp.zeros((EXTRA, TB), F32), out_ref)


def third_image_kernel(
    in_ref, hits_ref, scores_ref, first_ref, second_ref, state_ref, later_ref,
    out_ref, keep_ref,
):
    image = picked_sum(hits_ref[...], in_ref[...].reshape(COLS * MSG, TB))
    first = first_ref[...]
    old = second_ref[...] + later_ref[3:4, :] * first
    residual = scores_ref[...] - state_ref[2:3, :] * first - later_ref[2:3, :] * old
    keep_ref[0] = image
    keep_ref[1] = old
    keep_ref[2] = residual
    scalars = [lane_sum(image * residual), lane_sum(image * image), lane_sum(image * old)]
    extra = stack_rows(scalars)[:4]
    for i in range(ROWS):
        out_ref[i] = extra


def last_kernel(in_ref, keep_ref, image_ref, later_ref, weights_ref, residual_ref):
    total = added(in_ref)
    norm = total_of(total[0:1])
    ratio = norm / later_ref[0:1, :]
    image_norm = (
        total_of(total[1:2])
        + 2.0 * ratio * total_of(total[2:3])
        + ratio * ratio * later_ref[1:2, :]
    )
    step = norm / image_norm
    weights_ref[...] = keep_ref[2] + step * (keep_ref[0] + ratio * keep_ref[1])
    residual_ref[...] = image_ref[2] - step * (image_ref[0] + ratio * image_ref[1])


def call(kernel, outs, args, picked=False):
    def spec(x):
        scalar = x.dtype == jnp.int32
        return pl.BlockSpec(memory_space=pltpu.SMEM if scalar else pltpu.VMEM)

    return pl.pallas_call(
        kernel,
        out_shape=[jax.ShapeDtypeStruct(s, d) for s, d in outs],
        in_specs=[spec(a) for a in args],
        out_specs=[pl.BlockSpec(memory_space=pltpu.VMEM) for _ in outs],
        scratch_shapes=[pltpu.VMEM((CAP, TB), F32)] if picked else [],
        compiler_params=pltpu.CompilerParams(vmem_limit_bytes=16 * 2**20),
        name=kernel.__name__,
    )(*args)


def swap(x, axes):
    return lax.all_to_all(x, axes, 0, 0, tiled=True)


def local(tiles, tile_row, tile_col, tile_counts, scores):
    f = lambda *shape: (shape, F32)
    b = lambda *shape: (shape, BF16)
    cols = ("x", "core")
    to_z, to_y = f(Z, MSG, TB), f(Y, HAND, TB)
    to_cols = f(COLS, MSG, TB)
    image_shape, state_shape = f(ROW_BLOCKS, TB), f(EXTRA, TB)

    message, split = call(
        first_kernel,
        [to_z, b(CAP, 2 * TB, TB)],
        [tile_row, tile_col, tile_counts, tiles, scores],
        True,
    )
    (message,) = call(relay_kernel, [f(Y, LINE + EXTRA, TB)], [swap(message, "z")])
    message, first, hand_hits = call(
        gathered_kernel,
        [to_cols, f(WANT, TB), b(Y * WANT, LINE)],
        [tile_row, tile_counts, swap(message, "y"), split],
    )
    message, image, row_hits = call(
        first_image_kernel,
        [to_z, image_shape, b(ROW_BLOCKS, COLS * MSG)],
        [tile_row, tile_counts, swap(message, cols), split, scores],
        True,
    )
    (message,) = call(hand_kernel, [to_y], [swap(message, "z"), hand_hits])
    message, product, second, state = call(
        second_gradient_kernel,
        [to_cols, f(WANT, TB), f(WANT, TB), state_shape],
        [tile_counts, swap(message, "y"), split, first],
    )
    message, second_image = call(
        second_image_kernel,
        [to_z, image_shape],
        [tile_row, tile_counts, swap(message, cols), split, row_hits, scores, image, state],
        True,
    )
    (message,) = call(hand_kernel, [to_y], [swap(message, "z"), hand_hits])
    message, keep, later = call(
        third_gradient_kernel,
        [to_cols, f(3, SHARE, TB), state_shape],
        [tile_counts, swap(message, "y"), split, first, second, product, state],
    )
    message, images = call(
        third_image_kernel,
        [f(ROWS, 4, TB), f(3, ROW_BLOCKS, TB)],
        [swap(message, cols), row_hits, scores, image, second_image, state, later],
    )
    weights, residual = call(
        last_kernel,
        [f(SHARE, TB), image_shape],
        [swap(message, ("z", "y")), keep, images, later],
    )
    return weights, residual


def solution(mesh):
    fine = Mesh(mesh.devices.reshape(Z, Y, X, CORE), ("z", "y", "x", "core"))
    every = ("z", "y", "x", "core")
    return jax.shard_map(
        local,
        mesh=fine,
        in_specs=(P(every, None, None), P(every), P(every), P(every), P(("z", "y"), None)),
        out_specs=(P(("x", "core", "z", "y"), None), P(("z", "y"), None)),
        check_vma=False,
    )
```

time: 1610 us -> 178 us (0.11)
  waiting for transfers between devices: 1010 us -> 0 us
  blocking collectives: 537 us -> 164 us
  between operations: 21.7 us -> 1.35 us
  other arithmetic: 16.9 us -> 0 us
    psum x6 -> x0, waiting for transfers between devices: 1010 us -> none  [the longest x3 782 us: gradient_of(): return lax.psum(backward_partial(vector), 'rows')]
    psum x5 -> x0, blocking collectives: 537 us -> none  [the longest x3 325 us: norm_of(): return lax.psum(jnp.sum(piece * piece), ('rows', 'cols'))]
    all_to_all x0 -> x10, blocking collectives: none -> 164 us  [swap(): return lax.all_to_all(x, axes, 0, 0, tiled=True)]
  transfers between devices with their start and end apart: 6 -> 0, of which waited for: 6 -> 0; matrix products, arithmetic and copies ran while one was open for 0% -> 0% of each run, Pallas kernels for 0% -> 0%
where the time goes in v1:
time: 178 us; the launch traced here: 176 us
  blocking collectives  164 us (92%)
  Pallas kernels  7.37 us (4%)
  local copies, waits for them, and re-layouts  3.63 us (2%)
    all_to_all x10, blocking collectives, swap(): return lax.all_to_all(x, axes, 0, 0, tiled=True)  164 us
    pallas_call x11, Pallas kernels, call(): pl.pallas_call(kernel, out_shape=[jax.ShapeDtypeStruct(s, d) for s, d in...  7.37 us
    unnamed x12, local copies, waits for them, and re-layouts  3.63 us

profile of v1, /device:TPU:1, one launch (start us, length us, event | category | flops | bytes accessed | tf_op | source)
XLA Modules:
  0.0 176.1 jit_solution(4239379755157305766)
XLA Ops:
  1.3 0.0 copy-start
  1.3 0.9 copy-done
  2.2 0.0 copy-start.2
  2.2 1.4 copy-done.2
  3.6 0.0 copy-start.3
  3.6 0.7 copy-done.3
  4.2 0.0 copy-start.5
  4.3 0.7 copy-done.5
  4.9 1.0 first_kernel.1
  5.9 0.0 copy-start.4
  5.9 28.7 %all_to_all.50.in_ref = f32[16,32,128]{2,1,0:T(8,128)S(1)} all-to-all(f32[16,32,128]{2,1,0:T(8,128)S(1)} %get-tuple-element.21), channel_id=1, replica_groups=mesh['z'=16,'y'=4,'x'=4,'core'=2] {'z'}, dimensions={0} | all-to-all | bytes 524288 | tf_op jit(solution)/shard_map/all_to_all | solution.py:309
  34.6 0.1 relay_kernel.1
  34.7 12.4 %all_to_all.51.in_ref = f32[4,392,128]{2,1,0:T(8,128)S(1)} all-to-all(f32[4,392,128]{2,1,0:T(8,128)S(1)} %relay_kernel.1), channel_id=1, replica_groups=mesh['z'=16,'y'=4,'x'=4,'core'=2] {'y'}, dimensions={0} | all-to-all | bytes 1605632 | tf_op jit(solution)/shard_map/all_to_all | solution.py:309
  47.1 0.0 copy-start.1
  47.1 0.0 copy-done.4
  47.1 1.4 gathered_kernel.1
  48.5 17.0 %all_to_all.52.in_ref = f32[8,32,128]{2,1,0:T(8,128)S(1)} all-to-all(f32[8,32,128]{2,1,0:T(8,128)S(1)} %get-tuple-element.23), channel_id=1, replica_groups=mesh['z'=16,'y'=4,'x'=4,'core'=2] {'x','core'}, dimensions={0} | all-to-all | bytes 262144 | tf_op jit(solution)/shard_map/all_to_all | solution.py:309
  65.5 0.0 copy-done.1
  65.5 1.1 first_image_kernel.1
  66.6 21.1 %all_to_all.53.in_ref = f32[16,32,128]{2,1,0:T(8,128)S(1)} all-to-all(f32[16,32,128]{2,1,0:T(8,128)S(1)} %get-tuple-element.24), channel_id=1, replica_groups=mesh['z'=16,'y'=4,'x'=4,'core'=2] {'z'}, dimensions={0} | all-to-all | bytes 524288 | tf_op jit(solution)/shard_map/all_to_all | solution.py:309
  87.8 0.2 hand_kernel.2
  88.0 7.0 %all_to_all.54.in_ref = f32[4,48,128]{2,1,0:T(8,128)S(1)} all-to-all(f32[4,48,128]{2,1,0:T(8,128)S(1)} %hand_kernel.2), channel_id=1, replica_groups=mesh['z'=16,'y'=4,'x'=4,'core'=2] {'y'}, dimensions={0} | all-to-all | bytes 196608 | tf_op jit(solution)/shard_map/all_to_all | solution.py:309
  95.0 0.6 second_gradient_kernel.1
  95.6 15.3 %all_to_all.55.in_ref = f32[8,32,128]{2,1,0:T(8,128)S(1)} all-to-all(f32[8,32,128]{2,1,0:T(8,128)S(1)} %get-tuple-element.27), channel_id=1, replica_groups=mesh['z'=16,'y'=4,'x'=4,'core'=2] {'x','core'}, dimensions={0} | all-to-all | bytes 262144 | tf_op jit(solution)/shard_map/all_to_all | solution.py:309
  110.9 1.1 second_image_kernel.1
  112.0 18.1 %all_to_all.56.in_ref = f32[16,32,128]{2,1,0:T(8,128)S(1)} all-to-all(f32[16,32,128]{2,1,0:T(8,128)S(1)} %get-tuple-element.31), channel_id=1, replica_groups=mesh['z'=16,'y'=4,'x'=4,'core'=2] {'z'}, dimensions={0} | all-to-all | bytes 524288 | tf_op jit(solution)/shard_map/all_to_all | solution.py:309
  130.2 0.2 hand_kernel.3
  130.4 7.0 %all_to_all.57.in_ref = f32[4,48,128]{2,1,0:T(8,128)S(1)} all-to-all(f32[4,48,128]{2,1,0:T(8,128)S(1)} %hand_kernel.3), channel_id=1, replica_groups=mesh['z'=16,'y'=4,'x'=4,'core'=2] {'y'}, dimensions={0} | all-to-all | bytes 196608 | tf_op jit(solution)/shard_map/all_to_all | solution.py:309
  137.4 0.6 third_gradient_kernel.1
  138.0 15.3 %all_to_all.58.in_ref = f32[8,32,128]{2,1,0:T(8,128)S(1)} all-to-all(f32[8,32,128]{2,1,0:T(8,128)S(1)} %get-tuple-element.34), channel_id=1, replica_groups=mesh['z'=16,'y'=4,'x'=4,'core'=2] {'x','core'}, dimensions={0} | all-to-all | bytes 262144 | tf_op jit(solution)/shard_map/all_to_all | solution.py:309
  153.3 0.2 third_image_kernel.1
  153.5 21.8 %all_to_all.59.in_ref = f32[64,4,128]{2,1,0:T(4,128)S(1)} all-to-all(f32[64,4,128]{2,1,0:T(4,128)S(1)} %get-tuple-element.37), channel_id=1, replica_groups=mesh['z'=16,'y'=4,'x'=4,'core'=2] {'z','y'}, dimensions={0} | all-to-all | bytes 262144 | tf_op jit(solution)/shard_map/all_to_all | solution.py:309
  175.3 0.8 last_kernel.1
Async XLA Ops:
  1.3 0.9 copy-start
  2.2 1.4 copy-start.2
  3.6 0.7 copy-start.3
  4.2 0.7 copy-start.5
  5.9 41.2 %copy-start.4 = (s32[24]{0:T(128)S(1)}, s32[24]{0:T(128)}, u32[]{:S(2)}) copy-start(s32[24]{0:T(128)} %row_ref.7) | copy-start | bytes 292
  47.1 18.4 %copy-start.1 = (f32[256,128]{1,0:T(8,128)S(1)}, f32[256,128]{1,0:T(8,128)}, u32[]{:S(2)}) copy-start(f32[256,128]{1,0:T(8,128)} %scores_ref.7) | copy-start | bytes 393220

commit v2 on v1

v2 whole, which is shorter than its diff:
```python
import functools

import jax
import jax.numpy as jnp
from jax import lax
from jax.experimental import pallas as pl
from jax.experimental.pallas import tpu as pltpu
from jax.sharding import Mesh, PartitionSpec as P


Z, Y, X, CORE = 16, 4, 4, 2
COLS = X * CORE
ROWS = Z * Y
CAP = 24
TB = 128
ROW_BLOCKS = 256
SHARE = 16
WANT = CAP + SHARE
EXTRA = 8
MSG = CAP + 1
LINE = Z * MSG
SIDE = COLS * MSG
HAND = WANT + EXTRA
PARTS = 3
F32 = jnp.float32
BF16 = jnp.bfloat16


def iota(shape, dim):
    return lax.broadcasted_iota(jnp.int32, shape, dim)


def two_parts(x):
    high = x.astype(BF16).astype(F32)
    return high, x - high


def side_by_side(x):
    high, low = two_parts(x)
    return jnp.concatenate([high, low], axis=1).astype(BF16)


def picked_sum(hits, values):
    out = jnp.dot(hits, side_by_side(values), preferred_element_type=F32)
    return out[:, :TB] + out[:, TB:]


def times_tiles(vectors, split_ref, live, transposed):
    sub = iota((8, TB), 0)
    groups = []
    for g in range(CAP // 8):
        high, low = two_parts(vectors[8 * g : 8 * g + 8])
        both = jnp.concatenate([high, low], axis=0).astype(BF16)
        if transposed:
            both = jnp.concatenate([both, both], axis=1)
        total = jnp.zeros((8, TB), F32)
        for k in range(8):
            tile = split_ref[8 * g + k]
            if transposed:
                out = jnp.dot(both, tile, preferred_element_type=F32)
            else:
                out = lax.dot_general(
                    both, tile, (((1,), (1,)), ((), ())), preferred_element_type=F32
                )
                out = out[:, :TB] + out[:, TB:]
            total = jnp.where(sub == k, out[:8] + out[8:], total)
        groups.append(jnp.where(sub + 8 * g < live, total, 0.0))
    return jnp.concatenate(groups, axis=0)


def pick_rows(source, row_ref, picked):
    for j in range(CAP):
        picked[j : j + 1, :] = source[pl.ds(row_ref[j], 1), :]


def hits_of(wanted, lane_rows, width):
    pieces = [jnp.where(wanted == row, 1.0, 0.0) for row in lane_rows]
    return jnp.concatenate(pieces, axis=1)[:, :width].astype(BF16)


def index_row(index_ref, live, base):
    lane = iota((1, TB), 1)
    row = jnp.zeros((1, TB), F32)
    for j in range(CAP):
        value = jnp.where(j < live, index_ref[j] + 1, 0).astype(F32)
        row = jnp.where(lane == lax.rem(base + j, TB), value, row)
    return row


def index_lanes(in_ref, count):
    lane = iota((1, TB), 1)
    rows = []
    for k in range(-(-count * MSG // TB)):
        row = jnp.zeros((1, TB), F32)
        for i in range(count):
            low, high = MSG * i - TB * k, MSG * i + CAP - TB * k
            if high > 0 and low < TB:
                mine = (lane >= low) & (lane < high)
                row = jnp.where(mine, in_ref[MSG * i + CAP : MSG * (i + 1), :], row)
        rows.append(row)
    return rows


def send_to_all(out_ref, count, sums, row):
    message = jnp.concatenate([sums, row], axis=0)
    for i in range(count):
        out_ref[MSG * i : MSG * (i + 1), :] = message


def extra_sum(in_ref, count):
    row = in_ref[CAP : CAP + 1, :]
    for i in range(1, count):
        row = row + in_ref[MSG * i + CAP : MSG * (i + 1), :]
    return row


def scalar_row(rows):
    sums = jnp.sum(stack_rows(rows), axis=1, keepdims=True)
    apart = jnp.where(iota((EXTRA, TB), 0) == iota((EXTRA, TB), 1), sums, 0.0)
    return jnp.sum(apart, axis=0, keepdims=True)


def scalars_of(row, count):
    apart = jnp.where(iota((EXTRA, TB), 0) == iota((EXTRA, TB), 1), row, 0.0)
    sums = jnp.sum(apart, axis=1, keepdims=True)
    return [sums[k : k + 1] for k in range(count)]


def lane_sum(x):
    return jnp.sum(x, axis=0, keepdims=True)


def stack_rows(rows):
    sub = iota((EXTRA, TB), 0)
    out = jnp.zeros((EXTRA, TB), F32)
    for k, row in enumerate(rows):
        out = jnp.where(sub == k, row, out)
    return out


def first_kernel(
    row_hbm, col_hbm, live_hbm, tiles_hbm, scores_hbm, out_ref, split_ref,
    row_ref, col_ref, live_ref, tiles, scores, picked, done,
):
    part = CAP // PARTS
    copies = [
        pltpu.make_async_copy(row_hbm, row_ref, done.at[0]),
        pltpu.make_async_copy(col_hbm, col_ref, done.at[1]),
        pltpu.make_async_copy(live_hbm, live_ref, done.at[2]),
        pltpu.make_async_copy(scores_hbm, scores, done.at[3]),
    ]
    for i in range(PARTS):
        some = pl.ds(part * i, part)
        copies.append(pltpu.make_async_copy(tiles_hbm.at[some], tiles.at[some], done.at[4 + i]))
    for copy in copies:
        copy.start()
    for copy in copies[:4]:
        copy.wait()
    live = live_ref[0]
    pick_rows(scores, row_ref, picked)
    row = index_row(col_ref, live, lax.axis_index("z") * MSG)
    for i in range(PARTS):
        copies[4 + i].wait()
        for j in range(part * i, part * (i + 1)):
            high, low = two_parts(tiles[j])
            split_ref[j, :TB, :] = high.astype(BF16)
            split_ref[j, TB:, :] = low.astype(BF16)
    sums = times_tiles(picked[...], split_ref, live, True)
    send_to_all(out_ref, Z, sums, row)


def relay_kernel(in_ref, out_ref):
    rows = index_lanes(in_ref, Z)
    for y in range(Y):
        out_ref[y, :LINE, :] = in_ref[...]
        out_ref[y, LINE:, :] = stack_rows(rows)


def send_forward(vectors, split_ref, live, row, out_ref):
    send_to_all(out_ref, COLS, times_tiles(vectors, split_ref, live, False), row)


def gathered_kernel(row_ref, live_ref, in_ref, split_ref, out_ref, gradient_ref, hits_ref):
    live = live_ref[0]
    z, y = lax.axis_index("z"), lax.axis_index("y")
    lines = -(-LINE // TB)
    index = [[in_ref[i, LINE + k : LINE + k + 1, :] for k in range(lines)] for i in range(Y)]
    own_rows = index[0]
    for i in range(1, Y):
        own_rows = [jnp.where(y == i, new, old) for new, old in zip(index[i], own_rows)]
    own_wanted = jnp.zeros((WANT, 1), F32)
    lane, sub = iota((CAP, TB), 1), iota((CAP, TB), 0)
    for i in range(Y):
        found = jnp.zeros((CAP, TB), F32)
        for k in range(lines):
            found = jnp.where(lane + k * TB == sub + z * MSG, index[i][k], found)
        tile_part = jnp.sum(found, axis=1, keepdims=True)
        share_part = ((z * Y + i) * SHARE + 1 + iota((SHARE, 1), 0)).astype(F32)
        wanted = jnp.concatenate([tile_part, share_part], axis=0)
        hits_ref[WANT * i : WANT * (i + 1), :] = hits_of(wanted, own_rows, LINE)
        own_wanted = jnp.where(y == i, wanted, own_wanted)
    gradient = jnp.zeros((WANT, TB), F32)
    for i in range(Y):
        gradient += picked_sum(hits_of(own_wanted, index[i], LINE), in_ref[i, :LINE, :])
    gradient_ref[...] = gradient
    place = lax.axis_index("x") * CORE + lax.axis_index("core")
    row = index_row(row_ref, live, place * MSG)
    send_forward(gradient[:CAP], split_ref, live, row, out_ref)


def send_backward(image_ref, row_ref, split_ref, live, scalars, out_ref, picked):
    pick_rows(image_ref, row_ref, picked)
    sums = times_tiles(picked[...], split_ref, live, True)
    send_to_all(out_ref, Z, sums, scalar_row(scalars))


def first_image_kernel(
    row_ref, live_ref, in_ref, split_ref, scores_ref, out_ref, image_ref, hits_ref, picked
):
    wanted = (iota((ROW_BLOCKS, 1), 0) + 1).astype(F32)
    hits = hits_of(wanted, index_lanes(in_ref, COLS), SIDE)
    hits_ref[...] = hits
    image = picked_sum(hits, in_ref[...])
    image_ref[...] = image
    scalars = [lane_sum(image * scores_ref[...]), lane_sum(image * image)]
    send_backward(image_ref, row_ref, split_ref, live_ref[0], scalars, out_ref, picked)


def hand_kernel(in_ref, hits_ref, out_ref):
    extra = jnp.broadcast_to(extra_sum(in_ref, Z), (EXTRA, TB))
    sums = picked_sum(hits_ref[...], in_ref[...])
    for i in range(Y):
        out_ref[i, :WANT, :] = sums[WANT * i : WANT * (i + 1)]
        out_ref[i, WANT:, :] = extra


def added(in_ref):
    total = in_ref[0]
    for i in range(1, in_ref.shape[0]):
        total = total + in_ref[i]
    return total


def second_gradient_kernel(
    live_ref, in_ref, split_ref, gradient_ref, out_ref, product_ref, next_ref, state_ref
):
    total = added(in_ref)
    product = total[:WANT]
    norm, image_norm = scalars_of(total[WANT : WANT + 1], 2)
    step = norm / image_norm
    following = gradient_ref[...] - step * product
    product_ref[...] = product
    next_ref[...] = following
    state_ref[...] = stack_rows([norm, image_norm, step])
    send_forward(
        following[:CAP], split_ref, live_ref[0], jnp.zeros((1, TB), F32), out_ref
    )


def second_image_kernel(
    row_ref, live_ref, in_ref, split_ref, hits_ref, scores_ref, old_ref, state_ref,
    out_ref, image_ref, picked,
):
    image = picked_sum(hits_ref[...], in_ref[...])
    image_ref[...] = image
    old = old_ref[...]
    residual = scores_ref[...] - state_ref[2:3, :] * old
    scalars = [lane_sum(image * residual), lane_sum(image * image), lane_sum(image * old)]
    send_backward(image_ref, row_ref, split_ref, live_ref[0], scalars, out_ref, picked)


def third_gradient_kernel(
    live_ref, in_ref, split_ref, first_ref, second_ref, product_ref, state_ref,
    out_ref, keep_ref, later_ref,
):
    total = added(in_ref)
    old_norm, old_image_norm, old_step = state_ref[0:1, :], state_ref[1:2, :], state_ref[2:3, :]
    norm, straight, cross = scalars_of(total[WANT : WANT + 1], 3)
    ratio = norm / old_norm
    image_norm = straight + 2.0 * ratio * cross + ratio * ratio * old_image_norm
    step = norm / image_norm
    first, second = first_ref[...], second_ref[...]
    product = total[:WANT] + ratio * product_ref[...]
    third = second - step * product
    direction = second + ratio * first
    weights = old_step * first + step * direction
    keep_ref[0] = third[CAP:]
    keep_ref[1] = direction[CAP:]
    keep_ref[2] = weights[CAP:]
    later_ref[...] = stack_rows([norm, image_norm, step, ratio])
    send_forward(third[:CAP], split_ref, live_ref[0], jnp.zeros((1, TB), F32), out_ref)


def third_image_kernel(
    in_ref, hits_ref, scores_ref, first_ref, second_ref, state_ref, later_ref,
    out_ref, keep_ref,
):
    image = picked_sum(hits_ref[...], in_ref[...])
    first = first_ref[...]
    old = second_ref[...] + later_ref[3:4, :] * first
    residual = scores_ref[...] - state_ref[2:3, :] * first - later_ref[2:3, :] * old
    keep_ref[0] = image
    keep_ref[1] = old
    keep_ref[2] = residual
    scalars = [lane_sum(image * residual), lane_sum(image * image), lane_sum(image * old)]
    out_ref[...] = jnp.broadcast_to(scalar_row(scalars), (ROWS, TB))


def last_kernel(in_ref, keep_ref, image_ref, later_ref, weights_ref, residual_ref):
    norm, straight, cross = scalars_of(lane_sum(in_ref[...]), 3)
    ratio = norm / later_ref[0:1, :]
    image_norm = straight + 2.0 * ratio * cross + ratio * ratio * later_ref[1:2, :]
    step = norm / image_norm
    weights_ref[...] = keep_ref[2] + step * (keep_ref[0] + ratio * keep_ref[1])
    residual_ref[...] = image_ref[2] - step * (image_ref[0] + ratio * image_ref[1])


def call(kernel, outs, args, scratch=(), memory=None, room=16 * 2**20):
    def spec(x):
        scalar = x.dtype == jnp.int32
        return pl.BlockSpec(memory_space=memory or (pltpu.SMEM if scalar else pltpu.VMEM))

    return pl.pallas_call(
        kernel,
        out_shape=[jax.ShapeDtypeStruct(s, d) for s, d in outs],
        in_specs=[spec(a) for a in args],
        out_specs=[pl.BlockSpec(memory_space=pltpu.VMEM) for _ in outs],
        scratch_shapes=list(scratch),
        compiler_params=pltpu.CompilerParams(vmem_limit_bytes=room),
        name=kernel.__name__,
    )(*args)


def swap(x, axes, count):
    shape = x.shape
    if len(shape) == 2:
        x = x.reshape(count, shape[0] // count, 1, TB)
    return lax.all_to_all(x, axes, 0, 0, tiled=True).reshape(shape)


def local(tiles, tile_row, tile_col, tile_counts, scores):
    f = lambda *shape: (shape, F32)
    b = lambda *shape: (shape, BF16)
    cols = ("x", "core")
    to_z, to_y = f(LINE, TB), f(Y, HAND, TB)
    to_cols = f(SIDE, TB)
    image_shape, state_shape = f(ROW_BLOCKS, TB), f(EXTRA, TB)
    picked = [pltpu.VMEM((CAP, TB), F32)]

    message, split = call(
        first_kernel,
        [to_z, b(CAP, 2 * TB, TB)],
        [tile_row, tile_col, tile_counts, tiles, scores],
        [
            pltpu.SMEM((CAP,), jnp.int32),
            pltpu.SMEM((CAP,), jnp.int32),
            pltpu.SMEM((1,), jnp.int32),
            pltpu.VMEM((CAP, TB, TB), F32),
            pltpu.VMEM((ROW_BLOCKS, TB), F32),
            *picked,
            pltpu.SemaphoreType.DMA((4 + PARTS,)),
        ],
        pltpu.HBM,
        62 * 2**20,
    )
    (message,) = call(relay_kernel, [f(Y, LINE + EXTRA, TB)], [swap(message, "z", Z)])
    message, first, hand_hits = call(
        gathered_kernel,
        [to_cols, f(WANT, TB), b(Y * WANT, LINE)],
        [tile_row, tile_counts, swap(message, "y", Y), split],
    )
    message, image, row_hits = call(
        first_image_kernel,
        [to_z, image_shape, b(ROW_BLOCKS, SIDE)],
        [tile_row, tile_counts, swap(message, cols, COLS), split, scores],
        picked,
    )
    (message,) = call(hand_kernel, [to_y], [swap(message, "z", Z), hand_hits])
    message, product, second, state = call(
        second_gradient_kernel,
        [to_cols, f(WANT, TB), f(WANT, TB), state_shape],
        [tile_counts, swap(message, "y", Y), split, first],
    )
    message, second_image = call(
        second_image_kernel,
        [to_z, image_shape],
        [tile_row, tile_counts, swap(message, cols, COLS), split, row_hits, scores, image, state],
        picked,
    )
    (message,) = call(hand_kernel, [to_y], [swap(message, "z", Z), hand_hits])
    message, keep, later = call(
        third_gradient_kernel,
        [to_cols, f(3, SHARE, TB), state_shape],
        [tile_counts, swap(message, "y", Y), split, first, second, product, state],
    )
    message, images = call(
        third_image_kernel,
        [f(ROWS, TB), f(3, ROW_BLOCKS, TB)],
        [swap(message, cols, COLS), row_hits, scores, image, second_image, state, later],
    )
    weights, residual = call(
        last_kernel,
        [f(SHARE, TB), image_shape],
        [swap(message, ("z", "y"), ROWS), keep, images, later],
    )
    return weights, residual


def solution(mesh):
    fine = Mesh(mesh.devices.reshape(Z, Y, X, CORE), ("z", "y", "x", "core"))
    every = ("z", "y", "x", "core")
    return jax.shard_map(
        local,
        mesh=fine,
        in_specs=(P(every, None, None), P(every), P(every), P(every), P(("z", "y"), None)),
        out_specs=(P(("x", "core", "z", "y"), None), P(("z", "y"), None)),
        check_vma=False,
    )
```

time: 178 us -> 166 us (0.933)
  blocking collectives: 164 us -> 155 us
  local copies, waits for them, and re-layouts: 3.63 us -> 0.01 us
  Pallas kernels: 7.37 us -> 9.35 us
    all_to_all x10, blocking collectives: 164 us -> 155 us  [swap(): return lax.all_to_all(x, axes, 0, 0, tiled=True).reshape(shape)]
    unnamed x12 -> x6, local copies, waits for them, and re-layouts: 3.63 us -> 0.01 us
    pallas_call x11, Pallas kernels: 7.37 us -> 9.35 us  [call(): pl.pallas_call(kernel, out_shape=[jax.ShapeDtypeStruct(s, d) for s, d in...]
where the time goes in v2:
time: 166 us; the launch traced here: 165 us
  blocking collectives  155 us (93%)
  Pallas kernels  9.35 us (6%)
    all_to_all x10, blocking collectives, swap(): return lax.all_to_all(x, axes, 0, 0, tiled=True).reshape(shape)  155 us
    pallas_call x11, Pallas kernels, call(): pl.pallas_call(kernel, out_shape=[jax.ShapeDtypeStruct(s, d) for s, d in...  9.35 us

profile of v2, /device:TPU:1, one launch (start us, length us, event | category | flops | bytes accessed | tf_op | source)
XLA Modules:
  0.0 165.4 jit_solution(10749984556356045609)
XLA Ops:
  1.3 3.0 %first_kernel.1 = (f32[400,128]{1,0:T(8,128)}, bf16[24,256,128]{2,1,0:T(8,128)(2,1)}) custom-call(s32[24]{0:T(128)} %row_ref.5, s32[24]{0:T(128)} %col_hbm.1, s32[1]{0:T(128)S(6)} %copy.14.live_hbm.live_ref, f32[24,128,128]{2,1,0:T(8,128)} %tiles_hbm.1, f32[256,128]{1,0:T(8,128)} %scores_ref.5), custom_call_target="tpu_custom_call" | custom-call | tf_op jit(solution)/shard_map/first_kernel/pallas_call | solution.py:323
  4.3 0.0 copy-start
  4.3 0.0 copy-start.2
  4.3 28.5 %all_to_all.50 = f32[16,25,1,128]{3,2,1,0:T(1,128)S(1)} all-to-all(f32[16,25,1,128]{3,2,1,0:T(1,128)} %bitcast.29), channel_id=1, replica_groups=mesh['z'=16,'y'=4,'x'=4,'core'=2] {'z'}, dimensions={0} | all-to-all | bytes 409600 | tf_op jit(solution)/shard_map/all_to_all | solution.py:338
  32.7 0.1 relay_kernel.1
  32.8 12.6 %all_to_all.51.in_ref = f32[4,408,128]{2,1,0:T(8,128)S(1)} all-to-all(f32[4,408,128]{2,1,0:T(8,128)S(1)} %relay_kernel.1), channel_id=1, replica_groups=mesh['z'=16,'y'=4,'x'=4,'core'=2] {'y'}, dimensions={0} | all-to-all | bytes 1671168 | tf_op jit(solution)/shard_map/all_to_all | solution.py:338
  45.4 0.0 copy-start.1
  45.4 0.0 copy-done
  45.4 0.0 copy-done.2
  45.4 1.4 gathered_kernel.1
  46.8 15.6 %all_to_all.52 = f32[8,25,1,128]{3,2,1,0:T(1,128)S(1)} all-to-all(f32[8,25,1,128]{3,2,1,0:T(1,128)S(1)} %bitcast.27), channel_id=1, replica_groups=mesh['z'=16,'y'=4,'x'=4,'core'=2] {'x','core'}, dimensions={0} | all-to-all | bytes 204800 | tf_op jit(solution)/shard_map/all_to_all | solution.py:338
  62.4 0.0 copy-done.1
  62.4 1.1 first_image_kernel.1
  63.5 20.0 %all_to_all.53 = f32[16,25,1,128]{3,2,1,0:T(1,128)S(1)} all-to-all(f32[16,25,1,128]{3,2,1,0:T(1,128)S(1)} %bitcast.22), channel_id=1, replica_groups=mesh['z'=16,'y'=4,'x'=4,'core'=2] {'z'}, dimensions={0} | all-to-all | bytes 409600 | tf_op jit(solution)/shard_map/all_to_all | solution.py:338
  83.6 0.2 hand_kernel.2
  83.8 7.0 %all_to_all.54.in_ref = f32[4,48,128]{2,1,0:T(8,128)S(1)} all-to-all(f32[4,48,128]{2,1,0:T(8,128)S(1)} %hand_kernel.2), channel_id=1, replica_groups=mesh['z'=16,'y'=4,'x'=4,'core'=2] {'y'}, dimensions={0} | all-to-all | bytes 196608 | tf_op jit(solution)/shard_map/all_to_all | solution.py:338
  90.8 0.6 second_gradient_kernel.1
  91.4 13.7 %all_to_all.55 = f32[8,25,1,128]{3,2,1,0:T(1,128)S(1)} all-to-all(f32[8,25,1,128]{3,2,1,0:T(1,128)S(1)} %bitcast.26), channel_id=1, replica_groups=mesh['z'=16,'y'=4,'x'=4,'core'=2] {'x','core'}, dimensions={0} | all-to-all | bytes 204800 | tf_op jit(solution)/shard_map/all_to_all | solution.py:338
  105.1 1.1 second_image_kernel.1
  106.3 17.0 %all_to_all.56 = f32[16,25,1,128]{3,2,1,0:T(1,128)S(1)} all-to-all(f32[16,25,1,128]{3,2,1,0:T(1,128)S(1)} %bitcast.23), channel_id=1, replica_groups=mesh['z'=16,'y'=4,'x'=4,'core'=2] {'z'}, dimensions={0} | all-to-all | bytes 409600 | tf_op jit(solution)/shard_map/all_to_all | solution.py:338
  123.2 0.2 hand_kernel.3
  123.4 7.0 %all_to_all.57.in_ref = f32[4,48,128]{2,1,0:T(8,128)S(1)} all-to-all(f32[4,48,128]{2,1,0:T(8,128)S(1)} %hand_kernel.3), channel_id=1, replica_groups=mesh['z'=16,'y'=4,'x'=4,'core'=2] {'y'}, dimensions={0} | all-to-all | bytes 196608 | tf_op jit(solution)/shard_map/all_to_all | solution.py:338
  130.5 0.6 third_gradient_kernel.1
  131.1 13.7 %all_to_all.58 = f32[8,25,1,128]{3,2,1,0:T(1,128)S(1)} all-to-all(f32[8,25,1,128]{3,2,1,0:T(1,128)S(1)} %bitcast.25), channel_id=1, replica_groups=mesh['z'=16,'y'=4,'x'=4,'core'=2] {'x','core'}, dimensions={0} | all-to-all | bytes 204800 | tf_op jit(solution)/shard_map/all_to_all | solution.py:338
  144.8 0.3 third_image_kernel.1
  145.1 19.5 %all_to_all.59 = f32[64,1,1,128]{3,2,1,0:T(1,128)S(1)} all-to-all(f32[64,1,1,128]{3,2,1,0:T(1,128)S(1)} %bitcast.28), channel_id=1, replica_groups=mesh['z'=16,'y'=4,'x'=4,'core'=2] {'z','y'}, dimensions={0} | all-to-all | bytes 65536 | tf_op jit(solution)/shard_map/all_to_all | solution.py:338
  164.6 0.8 last_kernel.1
Async XLA Ops:
  4.3 41.1 %copy-start = (bf16[24,256,128]{2,1,0:T(8,128)(2,1)S(1)}, bf16[24,256,128]{2,1,0:T(8,128)(2,1)}, u32[]{:S(2)}) copy-start(bf16[24,256,128]{2,1,0:T(8,128)(2,1)} %get-tuple-element.22.split_ref) | copy-start | bytes 4718596
  4.3 41.1 %copy-start.2 = (s32[24]{0:T(128)S(1)}, s32[24]{0:T(128)}, u32[]{:S(2)}) copy-start(s32[24]{0:T(128)} %row_ref.5) | copy-start | bytes 292
  45.4 17.0 %copy-start.1 = (f32[256,128]{1,0:T(8,128)S(1)}, f32[256,128]{1,0:T(8,128)}, u32[]{:S(2)}) copy-start(f32[256,128]{1,0:T(8,128)} %scores_ref.5) | copy-start | bytes 393220

commit v3 on v2

--- a/solution.py
+++ b/solution.py
@@ -8,9 +8,10 @@
 from jax.sharding import Mesh, PartitionSpec as P
 
 
-Z, Y, X, CORE = 16, 4, 4, 2
+FAR, PAIR, Y, X, CORE = 8, 2, 4, 4, 2
+NEAR = PAIR * Y
 COLS = X * CORE
-ROWS = Z * Y
+ROWS = FAR * NEAR
 CAP = 24
 TB = 128
 ROW_BLOCKS = 256
@@ -18,7 +19,7 @@
 WANT = CAP + SHARE
 EXTRA = 8
 MSG = CAP + 1
-LINE = Z * MSG
+LINE = FAR * MSG
 SIDE = COLS * MSG
 HAND = WANT + EXTRA
 PARTS = 3
@@ -158,7 +159,7 @@
         copy.wait()
     live = live_ref[0]
     pick_rows(scores, row_ref, picked)
-    row = index_row(col_ref, live, lax.axis_index("z") * MSG)
+    row = index_row(col_ref, live, lax.axis_index("far") * MSG)
     for i in range(PARTS):
         copies[4 + i].wait()
         for j in range(part * i, part * (i + 1)):
@@ -166,14 +167,14 @@
             split_ref[j, :TB, :] = high.astype(BF16)
             split_ref[j, TB:, :] = low.astype(BF16)
     sums = times_tiles(picked[...], split_ref, live, True)
-    send_to_all(out_ref, Z, sums, row)
+    send_to_all(out_ref, FAR, sums, row)
 
 
 def relay_kernel(in_ref, out_ref):
-    rows = index_lanes(in_ref, Z)
-    for y in range(Y):
-        out_ref[y, :LINE, :] = in_ref[...]
-        out_ref[y, LINE:, :] = stack_rows(rows)
+    rows = index_lanes(in_ref, FAR)
+    for i in range(NEAR):
+        out_ref[i, :LINE, :] = in_ref[...]
+        out_ref[i, LINE:, :] = stack_rows(rows)
 
 
 def send_forward(vectors, split_ref, live, row, out_ref):
@@ -182,25 +183,26 @@
 
 def gathered_kernel(row_ref, live_ref, in_ref, split_ref, out_ref, gradient_ref, hits_ref):
     live = live_ref[0]
-    z, y = lax.axis_index("z"), lax.axis_index("y")
+    far = lax.axis_index("far")
+    near = lax.axis_index("pair") * Y + lax.axis_index("y")
     lines = -(-LINE // TB)
-    index = [[in_ref[i, LINE + k : LINE + k + 1, :] for k in range(lines)] for i in range(Y)]
+    index = [[in_ref[i, LINE + k : LINE + k + 1, :] for k in range(lines)] for i in range(NEAR)]
     own_rows = index[0]
-    for i in range(1, Y):
-        own_rows = [jnp.where(y == i, new, old) for new, old in zip(index[i], own_rows)]
+    for i in range(1, NEAR):
+        own_rows = [jnp.where(near == i, new, old) for new, old in zip(index[i], own_rows)]
     own_wanted = jnp.zeros((WANT, 1), F32)
     lane, sub = iota((CAP, TB), 1), iota((CAP, TB), 0)
-    for i in range(Y):
+    for i in range(NEAR):
         found = jnp.zeros((CAP, TB), F32)
         for k in range(lines):
-            found = jnp.where(lane + k * TB == sub + z * MSG, index[i][k], found)
+            found = jnp.where(lane + k * TB == sub + far * MSG, index[i][k], found)
         tile_part = jnp.sum(found, axis=1, keepdims=True)
-        share_part = ((z * Y + i) * SHARE + 1 + iota((SHARE, 1), 0)).astype(F32)
+        share_part = ((far * NEAR + i) * SHARE + 1 + iota((SHARE, 1), 0)).astype(F32)
         wanted = jnp.concatenate([tile_part, share_part], axis=0)
         hits_ref[WANT * i : WANT * (i + 1), :] = hits_of(wanted, own_rows, LINE)
-        own_wanted = jnp.where(y == i, wanted, own_wanted)
+        own_wanted = jnp.where(near == i, wanted, own_wanted)
     gradient = jnp.zeros((WANT, TB), F32)
-    for i in range(Y):
+    for i in range(NEAR):
         gradient += picked_sum(hits_of(own_wanted, index[i], LINE), in_ref[i, :LINE, :])
     gradient_ref[...] = gradient
     place = lax.axis_index("x") * CORE + lax.axis_index("core")
@@ -211,7 +213,7 @@
 def send_backward(image_ref, row_ref, split_ref, live, scalars, out_ref, picked):
     pick_rows(image_ref, row_ref, picked)
     sums = times_tiles(picked[...], split_ref, live, True)
-    send_to_all(out_ref, Z, sums, scalar_row(scalars))
+    send_to_all(out_ref, FAR, sums, scalar_row(scalars))
 
 
 def first_image_kernel(
@@ -227,9 +229,9 @@
 
 
 def hand_kernel(in_ref, hits_ref, out_ref):
-    extra = jnp.broadcast_to(extra_sum(in_ref, Z), (EXTRA, TB))
+    extra = jnp.broadcast_to(extra_sum(in_ref, FAR), (EXTRA, TB))
     sums = picked_sum(hits_ref[...], in_ref[...])
-    for i in range(Y):
+    for i in range(NEAR):
         out_ref[i, :WANT, :] = sums[WANT * i : WANT * (i + 1)]
         out_ref[i, WANT:, :] = extra
 
@@ -341,15 +343,15 @@
 def local(tiles, tile_row, tile_col, tile_counts, scores):
     f = lambda *shape: (shape, F32)
     b = lambda *shape: (shape, BF16)
-    cols = ("x", "core")
-    to_z, to_y = f(LINE, TB), f(Y, HAND, TB)
+    near, cols = ("pair", "y"), ("x", "core")
+    to_far, to_near = f(LINE, TB), f(NEAR, HAND, TB)
     to_cols = f(SIDE, TB)
     image_shape, state_shape = f(ROW_BLOCKS, TB), f(EXTRA, TB)
     picked = [pltpu.VMEM((CAP, TB), F32)]
 
     message, split = call(
         first_kernel,
-        [to_z, b(CAP, 2 * TB, TB)],
+        [to_far, b(CAP, 2 * TB, TB)],
         [tile_row, tile_col, tile_counts, tiles, scores],
         [
             pltpu.SMEM((CAP,), jnp.int32),
@@ -363,35 +365,35 @@
         pltpu.HBM,
         62 * 2**20,
     )
-    (message,) = call(relay_kernel, [f(Y, LINE + EXTRA, TB)], [swap(message, "z", Z)])
+    (message,) = call(relay_kernel, [f(NEAR, LINE + EXTRA, TB)], [swap(message, "far", FAR)])
     message, first, hand_hits = call(
         gathered_kernel,
-        [to_cols, f(WANT, TB), b(Y * WANT, LINE)],
-        [tile_row, tile_counts, swap(message, "y", Y), split],
+        [to_cols, f(WANT, TB), b(NEAR * WANT, LINE)],
+        [tile_row, tile_counts, swap(message, near, NEAR), split],
     )
     message, image, row_hits = call(
         first_image_kernel,
-        [to_z, image_shape, b(ROW_BLOCKS, SIDE)],
+        [to_far, image_shape, b(ROW_BLOCKS, SIDE)],
         [tile_row, tile_counts, swap(message, cols, COLS), split, scores],
         picked,
     )
-    (message,) = call(hand_kernel, [to_y], [swap(message, "z", Z), hand_hits])
+    (message,) = call(hand_kernel, [to_near], [swap(message, "far", FAR), hand_hits])
     message, product, second, state = call(
         second_gradient_kernel,
         [to_cols, f(WANT, TB), f(WANT, TB), state_shape],
-        [tile_counts, swap(message, "y", Y), split, first],
+        [tile_counts, swap(message, near, NEAR), split, first],
     )
     message, second_image = call(
         second_image_kernel,
-        [to_z, image_shape],
+        [to_far, image_shape],
         [tile_row, tile_counts, swap(message, cols, COLS), split, row_hits, scores, image, state],
         picked,
     )
-    (message,) = call(hand_kernel, [to_y], [swap(message, "z", Z), hand_hits])
+    (message,) = call(hand_kernel, [to_near], [swap(message, "far", FAR), hand_hits])
     message, keep, later = call(
         third_gradient_kernel,
         [to_cols, f(3, SHARE, TB), state_shape],
-        [tile_counts, swap(message, "y", Y), split, first, second, product, state],
+        [tile_counts, swap(message, near, NEAR), split, first, second, product, state],
     )
     message, images = call(
         third_image_kernel,
@@ -401,18 +403,19 @@
     weights, residual = call(
         last_kernel,
         [f(SHARE, TB), image_shape],
-        [swap(message, ("z", "y"), ROWS), keep, images, later],
+        [swap(message, ("far", *near), ROWS), keep, images, later],
     )
     return weights, residual
 
 
 def solution(mesh):
-    fine = Mesh(mesh.devices.reshape(Z, Y, X, CORE), ("z", "y", "x", "core"))
-    every = ("z", "y", "x", "core")
+    rows, cols = ("far", "pair", "y"), ("x", "core")
+    every = rows + cols
+    fine = Mesh(mesh.devices.reshape(FAR, PAIR, Y, X, CORE), every)
     return jax.shard_map(
         local,
         mesh=fine,
-        in_specs=(P(every, None, None), P(every), P(every), P(every), P(("z", "y"), None)),
-        out_specs=(P(("x", "core", "z", "y"), None), P(("z", "y"), None)),
+        in_specs=(P(every, None, None), P(every), P(every), P(every), P(rows, None)),
+        out_specs=(P(cols + rows, None), P(rows, None)),
         check_vma=False,
     )

time: 166 us -> 157 us (0.946)
  blocking collectives: 155 us -> 145 us
    all_to_all x10, blocking collectives: 155 us -> 145 us  [swap(): return lax.all_to_all(x, axes, 0, 0, tiled=True).reshape(shape)]
where the time goes in v3:
time: 157 us; the launch traced here: 156 us
  blocking collectives  145 us (92%)
  Pallas kernels  9.31 us (6%)
    all_to_all x10, blocking collectives, swap(): return lax.all_to_all(x, axes, 0, 0, tiled=True).reshape(shape)  145 us
    pallas_call x11, Pallas kernels, call(): pl.pallas_call(kernel, out_shape=[jax.ShapeDtypeStruct(s, d) for s, d in...  9.31 us

profile of v3, /device:TPU:1, one launch (start us, length us, event | category | flops | bytes accessed | tf_op | source)
XLA Modules:
  0.0 156.1 jit_solution(16895808388291038384)
XLA Ops:
  1.3 2.9 %first_kernel.1 = (f32[200,128]{1,0:T(8,128)}, bf16[24,256,128]{2,1,0:T(8,128)(2,1)}) custom-call(s32[24]{0:T(128)} %row_ref.5, s32[24]{0:T(128)} %col_hbm.1, s32[1]{0:T(128)S(6)} %copy.14.live_hbm.live_ref, f32[24,128,128]{2,1,0:T(8,128)} %tiles_hbm.1, f32[256,128]{1,0:T(8,128)} %scores_ref.5), custom_call_target="tpu_custom_call" | custom-call | tf_op jit(solution)/shard_map/first_kernel/pallas_call | solution.py:325
  4.2 0.0 copy-start
  4.2 0.0 copy-start.2
  4.2 28.4 %all_to_all.50 = f32[8,25,1,128]{3,2,1,0:T(1,128)S(1)} all-to-all(f32[8,25,1,128]{3,2,1,0:T(1,128)} %bitcast.29), channel_id=1, replica_groups=mesh['far'=8,'pair'=2,'y'=4,'x'=4,'core'=2] {'far'}, dimensions={0} | all-to-all | bytes 204800 | tf_op jit(solution)/shard_map/all_to_all | solution.py:340
  32.6 0.1 relay_kernel.1
  32.7 13.7 %all_to_all.51.in_ref = f32[8,208,128]{2,1,0:T(8,128)S(1)} all-to-all(f32[8,208,128]{2,1,0:T(8,128)S(1)} %relay_kernel.1), channel_id=1, replica_groups=mesh['far'=8,'pair'=2,'y'=4,'x'=4,'core'=2] {'pair','y'}, dimensions={0} | all-to-all | bytes 1703936 | tf_op jit(solution)/shard_map/all_to_all | solution.py:340
  46.4 0.0 copy-start.1
  46.4 0.0 copy-done
  46.4 0.0 copy-done.2
  46.4 1.5 gathered_kernel.1
  47.9 14.3 %all_to_all.52 = f32[8,25,1,128]{3,2,1,0:T(1,128)S(1)} all-to-all(f32[8,25,1,128]{3,2,1,0:T(1,128)S(1)} %bitcast.25), channel_id=1, replica_groups=mesh['far'=8,'pair'=2,'y'=4,'x'=4,'core'=2] {'x','core'}, dimensions={0} | all-to-all | bytes 204800 | tf_op jit(solution)/shard_map/all_to_all | solution.py:340
  62.2 0.0 copy-done.1
  62.2 1.1 first_image_kernel.1
  63.3 16.4 %all_to_all.53 = f32[8,25,1,128]{3,2,1,0:T(1,128)S(1)} all-to-all(f32[8,25,1,128]{3,2,1,0:T(1,128)S(1)} %bitcast.26), channel_id=1, replica_groups=mesh['far'=8,'pair'=2,'y'=4,'x'=4,'core'=2] {'far'}, dimensions={0} | all-to-all | bytes 204800 | tf_op jit(solution)/shard_map/all_to_all | solution.py:340
  79.7 0.2 hand_kernel.2
  79.9 8.2 %all_to_all.54.in_ref = f32[8,48,128]{2,1,0:T(8,128)S(1)} all-to-all(f32[8,48,128]{2,1,0:T(8,128)S(1)} %hand_kernel.2), channel_id=1, replica_groups=mesh['far'=8,'pair'=2,'y'=4,'x'=4,'core'=2] {'pair','y'}, dimensions={0} | all-to-all | bytes 393216 | tf_op jit(solution)/shard_map/all_to_all | solution.py:340
  88.1 0.6 second_gradient_kernel.1
  88.7 12.3 %all_to_all.55 = f32[8,25,1,128]{3,2,1,0:T(1,128)S(1)} all-to-all(f32[8,25,1,128]{3,2,1,0:T(1,128)S(1)} %bitcast.24), channel_id=1, replica_groups=mesh['far'=8,'pair'=2,'y'=4,'x'=4,'core'=2] {'x','core'}, dimensions={0} | all-to-all | bytes 204800 | tf_op jit(solution)/shard_map/all_to_all | solution.py:340
  101.0 1.1 second_image_kernel.1
  102.1 15.1 %all_to_all.56 = f32[8,25,1,128]{3,2,1,0:T(1,128)S(1)} all-to-all(f32[8,25,1,128]{3,2,1,0:T(1,128)S(1)} %bitcast.27), channel_id=1, replica_groups=mesh['far'=8,'pair'=2,'y'=4,'x'=4,'core'=2] {'far'}, dimensions={0} | all-to-all | bytes 204800 | tf_op jit(solution)/shard_map/all_to_all | solution.py:340
  117.1 0.2 hand_kernel.3
  117.3 8.2 %all_to_all.57.in_ref = f32[8,48,128]{2,1,0:T(8,128)S(1)} all-to-all(f32[8,48,128]{2,1,0:T(8,128)S(1)} %hand_kernel.3), channel_id=1, replica_groups=mesh['far'=8,'pair'=2,'y'=4,'x'=4,'core'=2] {'pair','y'}, dimensions={0} | all-to-all | bytes 393216 | tf_op jit(solution)/shard_map/all_to_all | solution.py:340
  125.5 0.6 third_gradient_kernel.1
  126.1 11.5 %all_to_all.58 = f32[8,25,1,128]{3,2,1,0:T(1,128)S(1)} all-to-all(f32[8,25,1,128]{3,2,1,0:T(1,128)S(1)} %bitcast.23), channel_id=1, replica_groups=mesh['far'=8,'pair'=2,'y'=4,'x'=4,'core'=2] {'x','core'}, dimensions={0} | all-to-all | bytes 204800 | tf_op jit(solution)/shard_map/all_to_all | solution.py:340
  137.6 0.3 third_image_kernel.1
  137.9 17.4 %all_to_all.59 = f32[64,1,1,128]{3,2,1,0:T(1,128)S(1)} all-to-all(f32[64,1,1,128]{3,2,1,0:T(1,128)S(1)} %bitcast.28), channel_id=1, replica_groups=mesh['far'=8,'pair'=2,'y'=4,'x'=4,'core'=2] {'far','pair','y'}, dimensions={0} | all-to-all | bytes 65536 | tf_op jit(solution)/shard_map/all_to_all | solution.py:340
  155.3 0.8 last_kernel.1
Async XLA Ops:
  4.2 42.2 %copy-start = (bf16[24,256,128]{2,1,0:T(8,128)(2,1)S(1)}, bf16[24,256,128]{2,1,0:T(8,128)(2,1)}, u32[]{:S(2)}) copy-start(bf16[24,256,128]{2,1,0:T(8,128)(2,1)} %get-tuple-element.22.split_ref) | copy-start | bytes 4718596
  4.2 42.2 %copy-start.2 = (s32[24]{0:T(128)S(1)}, s32[24]{0:T(128)}, u32[]{:S(2)}) copy-start(s32[24]{0:T(128)} %row_ref.5) | copy-start | bytes 292
  46.4 15.8 %copy-start.1 = (f32[256,128]{1,0:T(8,128)S(1)}, f32[256,128]{1,0:T(8,128)}, u32[]{:S(2)}) copy-start(f32[256,128]{1,0:T(8,128)} %scores_ref.5) | copy-start | bytes 393220

commit v4 on v3

--- a/solution.py
+++ b/solution.py
@@ -23,6 +23,7 @@
 SIDE = COLS * MSG
 HAND = WANT + EXTRA
 PARTS = 3
+INFO = 2 * CAP + EXTRA
 F32 = jnp.float32
 BF16 = jnp.bfloat16
 
@@ -65,8 +66,15 @@
                 )
                 out = out[:, :TB] + out[:, TB:]
             total = jnp.where(sub == k, out[:8] + out[8:], total)
-        groups.append(jnp.where(sub + 8 * g < live, total, 0.0))
+        groups.append(jnp.where(live[8 * g : 8 * g + 8] > 0.0, total, 0.0))
     return jnp.concatenate(groups, axis=0)
+
+
+def split_tiles(tiles, split_ref, start, stop):
+    for j in range(start, stop):
+        high, low = two_parts(tiles[j])
+        split_ref[j, :TB, :] = high.astype(BF16)
+        split_ref[j, TB:, :] = low.astype(BF16)
 
 
 def pick_rows(source, row_ref, picked):
@@ -140,8 +148,8 @@
 
 
 def first_kernel(
-    row_hbm, col_hbm, live_hbm, tiles_hbm, scores_hbm, out_ref, split_ref,
-    row_ref, col_ref, live_ref, tiles, scores, picked, done,
+    row_hbm, col_hbm, live_hbm, tiles_hbm, scores_hbm, out_ref, info_ref,
+    row_ref, col_ref, live_ref, tiles, scores, split_ref, picked, done,
 ):
     part = CAP // PARTS
     copies = [
@@ -160,13 +168,19 @@
     live = live_ref[0]
     pick_rows(scores, row_ref, picked)
     row = index_row(col_ref, live, lax.axis_index("far") * MSG)
+    sub = iota((CAP, TB), 0)
+    mask = jnp.where(sub < live, 1.0, 0.0)
+    own = jnp.full((CAP, TB), -1.0, F32)
+    for j in range(CAP):
+        own = jnp.where(sub == j, jnp.where(j < live, row_ref[j] + 1, -1).astype(F32), own)
+    place = lax.axis_index("x") * CORE + lax.axis_index("core")
+    info_ref[:CAP, :] = mask
+    info_ref[CAP : 2 * CAP, :] = own
+    info_ref[2 * CAP :, :] = stack_rows([index_row(row_ref, live, place * MSG)])
     for i in range(PARTS):
         copies[4 + i].wait()
-        for j in range(part * i, part * (i + 1)):
-            high, low = two_parts(tiles[j])
-            split_ref[j, :TB, :] = high.astype(BF16)
-            split_ref[j, TB:, :] = low.astype(BF16)
-    sums = times_tiles(picked[...], split_ref, live, True)
+        split_tiles(tiles, split_ref, part * i, part * (i + 1))
+    sums = times_tiles(picked[...], split_ref, mask, True)
     send_to_all(out_ref, FAR, sums, row)
 
 
@@ -177,12 +191,14 @@
         out_ref[i, LINE:, :] = stack_rows(rows)
 
 
-def send_forward(vectors, split_ref, live, row, out_ref):
-    send_to_all(out_ref, COLS, times_tiles(vectors, split_ref, live, False), row)
-
-
-def gathered_kernel(row_ref, live_ref, in_ref, split_ref, out_ref, gradient_ref, hits_ref):
-    live = live_ref[0]
+def send_forward(vectors, split_ref, info_ref, row, out_ref):
+    send_to_all(out_ref, COLS, times_tiles(vectors, split_ref, info_ref[:CAP, :], False), row)
+
+
+def gathered_kernel(
+    info_ref, in_ref, tiles_ref, out_ref, gradient_ref, hits_ref, split_ref
+):
+    split_tiles(tiles_ref, split_ref, 0, CAP)
     far = lax.axis_index("far")
     near = lax.axis_index("pair") * Y + lax.axis_index("y")
     lines = -(-LINE // TB)
@@ -197,6 +213,7 @@
         for k in range(lines):
             found = jnp.where(lane + k * TB == sub + far * MSG, index[i][k], found)
         tile_part = jnp.sum(found, axis=1, keepdims=True)
+        tile_part = jnp.where(tile_part == 0.0, -1.0, tile_part)
         share_part = ((far * NEAR + i) * SHARE + 1 + iota((SHARE, 1), 0)).astype(F32)
         wanted = jnp.concatenate([tile_part, share_part], axis=0)
         hits_ref[WANT * i : WANT * (i + 1), :] = hits_of(wanted, own_rows, LINE)
@@ -205,27 +222,26 @@
     for i in range(NEAR):
         gradient += picked_sum(hits_of(own_wanted, index[i], LINE), in_ref[i, :LINE, :])
     gradient_ref[...] = gradient
-    place = lax.axis_index("x") * CORE + lax.axis_index("core")
-    row = index_row(row_ref, live, place * MSG)
-    send_forward(gradient[:CAP], split_ref, live, row, out_ref)
-
-
-def send_backward(image_ref, row_ref, split_ref, live, scalars, out_ref, picked):
-    pick_rows(image_ref, row_ref, picked)
-    sums = times_tiles(picked[...], split_ref, live, True)
+    send_forward(gradient[:CAP], split_ref, info_ref, info_ref[2 * CAP : 2 * CAP + 1, :], out_ref)
+
+
+def send_backward(picked, split_ref, info_ref, scalars, out_ref):
+    sums = times_tiles(picked, split_ref, info_ref[:CAP, :], True)
     send_to_all(out_ref, FAR, sums, scalar_row(scalars))
 
 
 def first_image_kernel(
-    row_ref, live_ref, in_ref, split_ref, scores_ref, out_ref, image_ref, hits_ref, picked
+    info_ref, in_ref, split_ref, scores_ref, out_ref, image_ref, hits_ref
 ):
     wanted = (iota((ROW_BLOCKS, 1), 0) + 1).astype(F32)
+    wanted = jnp.concatenate([wanted, info_ref[CAP : 2 * CAP, :1]], axis=0)
     hits = hits_of(wanted, index_lanes(in_ref, COLS), SIDE)
     hits_ref[...] = hits
-    image = picked_sum(hits, in_ref[...])
+    sums = picked_sum(hits, in_ref[...])
+    image = sums[:ROW_BLOCKS]
     image_ref[...] = image
     scalars = [lane_sum(image * scores_ref[...]), lane_sum(image * image)]
-    send_backward(image_ref, row_ref, split_ref, live_ref[0], scalars, out_ref, picked)
+    send_backward(sums[ROW_BLOCKS:], split_ref, info_ref, scalars, out_ref)
 
 
 def hand_kernel(in_ref, hits_ref, out_ref):
@@ -244,7 +260,7 @@
 
 
 def second_gradient_kernel(
-    live_ref, in_ref, split_ref, gradient_ref, out_ref, product_ref, next_ref, state_ref
+    info_ref, in_ref, split_ref, gradient_ref, out_ref, product_ref, next_ref, state_ref
 ):
     total = added(in_ref)
     product = total[:WANT]
@@ -254,25 +270,23 @@
     product_ref[...] = product
     next_ref[...] = following
     state_ref[...] = stack_rows([norm, image_norm, step])
-    send_forward(
-        following[:CAP], split_ref, live_ref[0], jnp.zeros((1, TB), F32), out_ref
-    )
+    send_forward(following[:CAP], split_ref, info_ref, jnp.zeros((1, TB), F32), out_ref)
 
 
 def second_image_kernel(
-    row_ref, live_ref, in_ref, split_ref, hits_ref, scores_ref, old_ref, state_ref,
-    out_ref, image_ref, picked,
-):
-    image = picked_sum(hits_ref[...], in_ref[...])
+    info_ref, in_ref, split_ref, hits_ref, scores_ref, old_ref, state_ref, out_ref, image_ref
+):
+    sums = picked_sum(hits_ref[...], in_ref[...])
+    image = sums[:ROW_BLOCKS]
     image_ref[...] = image
     old = old_ref[...]
     residual = scores_ref[...] - state_ref[2:3, :] * old
     scalars = [lane_sum(image * residual), lane_sum(image * image), lane_sum(image * old)]
-    send_backward(image_ref, row_ref, split_ref, live_ref[0], scalars, out_ref, picked)
+    send_backward(sums[ROW_BLOCKS:], split_ref, info_ref, scalars, out_ref)
 
 
 def third_gradient_kernel(
-    live_ref, in_ref, split_ref, first_ref, second_ref, product_ref, state_ref,
+    info_ref, in_ref, split_ref, first_ref, second_ref, product_ref, state_ref,
     out_ref, keep_ref, later_ref,
 ):
     total = added(in_ref)
@@ -290,14 +304,14 @@
     keep_ref[1] = direction[CAP:]
     keep_ref[2] = weights[CAP:]
     later_ref[...] = stack_rows([norm, image_norm, step, ratio])
-    send_forward(third[:CAP], split_ref, live_ref[0], jnp.zeros((1, TB), F32), out_ref)
+    send_forward(third[:CAP], split_ref, info_ref, jnp.zeros((1, TB), F32), out_ref)
 
 
 def third_image_kernel(
     in_ref, hits_ref, scores_ref, first_ref, second_ref, state_ref, later_ref,
     out_ref, keep_ref,
 ):
-    image = picked_sum(hits_ref[...], in_ref[...])
+    image = picked_sum(hits_ref[:ROW_BLOCKS, :], in_ref[...])
     first = first_ref[...]
     old = second_ref[...] + later_ref[3:4, :] * first
     residual = scores_ref[...] - state_ref[2:3, :] * first - later_ref[2:3, :] * old
@@ -347,11 +361,10 @@
     to_far, to_near = f(LINE, TB), f(NEAR, HAND, TB)
     to_cols = f(SIDE, TB)
     image_shape, state_shape = f(ROW_BLOCKS, TB), f(EXTRA, TB)
-    picked = [pltpu.VMEM((CAP, TB), F32)]
-
-    message, split = call(
+
+    message, info = call(
         first_kernel,
-        [to_far, b(CAP, 2 * TB, TB)],
+        [to_far, f(INFO, TB)],
         [tile_row, tile_col, tile_counts, tiles, scores],
         [
             pltpu.SMEM((CAP,), jnp.int32),
@@ -359,41 +372,40 @@
             pltpu.SMEM((1,), jnp.int32),
             pltpu.VMEM((CAP, TB, TB), F32),
             pltpu.VMEM((ROW_BLOCKS, TB), F32),
-            *picked,
+            pltpu.VMEM((CAP, 2 * TB, TB), BF16),
+            pltpu.VMEM((CAP, TB), F32),
             pltpu.SemaphoreType.DMA((4 + PARTS,)),
         ],
         pltpu.HBM,
         62 * 2**20,
     )
     (message,) = call(relay_kernel, [f(NEAR, LINE + EXTRA, TB)], [swap(message, "far", FAR)])
-    message, first, hand_hits = call(
+    message, first, hand_hits, split = call(
         gathered_kernel,
-        [to_cols, f(WANT, TB), b(NEAR * WANT, LINE)],
-        [tile_row, tile_counts, swap(message, near, NEAR), split],
+        [to_cols, f(WANT, TB), b(NEAR * WANT, LINE), b(CAP, 2 * TB, TB)],
+        [info, swap(message, near, NEAR), tiles],
     )
     message, image, row_hits = call(
         first_image_kernel,
-        [to_far, image_shape, b(ROW_BLOCKS, SIDE)],
-        [tile_row, tile_counts, swap(message, cols, COLS), split, scores],
-        picked,
+        [to_far, image_shape, b(ROW_BLOCKS + CAP, SIDE)],
+        [info, swap(message, cols, COLS), split, scores],
     )
     (message,) = call(hand_kernel, [to_near], [swap(message, "far", FAR), hand_hits])
     message, product, second, state = call(
         second_gradient_kernel,
         [to_cols, f(WANT, TB), f(WANT, TB), state_shape],
-        [tile_counts, swap(message, near, NEAR), split, first],
+        [info, swap(message, near, NEAR), split, first],
     )
     message, second_image = call(
         second_image_kernel,
         [to_far, image_shape],
-        [tile_row, tile_counts, swap(message, cols, COLS), split, row_hits, scores, image, state],
-        picked,
+        [info, swap(message, cols, COLS), split, row_hits, scores, image, state],
     )
     (message,) = call(hand_kernel, [to_near], [swap(message, "far", FAR), hand_hits])
     message, keep, later = call(
         third_gradient_kernel,
         [to_cols, f(3, SHARE, TB), state_shape],
-        [tile_counts, swap(message, near, NEAR), split, first, second, product, state],
+        [info, swap(message, near, NEAR), split, first, second, product, state],
     )
     message, images = call(
         third_image_kernel,

time: 157 us -> 155 us (0.987)
  Pallas kernels: 9.31 us -> 7.31 us
    pallas_call x11, Pallas kernels: 9.31 us -> 7.31 us  [call(): pl.pallas_call(kernel, out_shape=[jax.ShapeDtypeStruct(s, d) for s, d in...]
where the time goes in v4:
time: 155 us; the launch traced here: 154 us
  blocking collectives  145 us (94%)
  Pallas kernels  7.31 us (5%)
    all_to_all x10, blocking collectives, swap(): return lax.all_to_all(x, axes, 0, 0, tiled=True).reshape(shape)  145 us
    pallas_call x11, Pallas kernels, call(): pl.pallas_call(kernel, out_shape=[jax.ShapeDtypeStruct(s, d) for s, d in...  7.31 us

profile of v4, /device:TPU:1, one launch (start us, length us, event | category | flops | bytes accessed | tf_op | source)
XLA Modules:
  0.0 154.1 jit_solution(10141017699306132505)
XLA Ops:
  1.3 2.5 %first_kernel.1 = (f32[200,128]{1,0:T(8,128)}, f32[56,128]{1,0:T(8,128)}) custom-call(s32[24]{0:T(128)} %row_hbm.1, s32[24]{0:T(128)} %col_hbm.1, s32[1]{0:T(128)S(6)} %copy.14.live_hbm, f32[24,128,128]{2,1,0:T(8,128)} %tiles_ref.1, f32[256,128]{1,0:T(8,128)} %scores_ref.5), custom_call_target="tpu_custom_call" | custom-call | tf_op jit(solution)/shard_map/first_kernel/pallas_call | solution.py:339
  3.8 0.0 copy-start
  3.8 0.0 copy-start.2
  3.8 28.4 %all_to_all.50 = f32[8,25,1,128]{3,2,1,0:T(1,128)S(1)} all-to-all(f32[8,25,1,128]{3,2,1,0:T(1,128)} %bitcast.29), channel_id=1, replica_groups=mesh['far'=8,'pair'=2,'y'=4,'x'=4,'core'=2] {'far'}, dimensions={0} | all-to-all | bytes 204800 | tf_op jit(solution)/shard_map/all_to_all | solution.py:354
  32.3 0.1 relay_kernel.1
  32.3 13.7 %all_to_all.51.in_ref = f32[8,208,128]{2,1,0:T(8,128)S(1)} all-to-all(f32[8,208,128]{2,1,0:T(8,128)S(1)} %relay_kernel.1), channel_id=1, replica_groups=mesh['far'=8,'pair'=2,'y'=4,'x'=4,'core'=2] {'pair','y'}, dimensions={0} | all-to-all | bytes 1703936 | tf_op jit(solution)/shard_map/all_to_all | solution.py:354
  46.0 0.0 copy-start.1
  46.0 0.0 copy-done
  46.0 0.0 copy-done.2
  46.0 0.9 gathered_kernel.1
  47.0 14.3 %all_to_all.52 = f32[8,25,1,128]{3,2,1,0:T(1,128)S(1)} all-to-all(f32[8,25,1,128]{3,2,1,0:T(1,128)S(1)} %bitcast.24), channel_id=1, replica_groups=mesh['far'=8,'pair'=2,'y'=4,'x'=4,'core'=2] {'x','core'}, dimensions={0} | all-to-all | bytes 204800 | tf_op jit(solution)/shard_map/all_to_all | solution.py:354
  61.2 0.0 copy-done.1
  61.2 0.6 first_image_kernel.1
  61.8 16.4 %all_to_all.53 = f32[8,25,1,128]{3,2,1,0:T(1,128)S(1)} all-to-all(f32[8,25,1,128]{3,2,1,0:T(1,128)S(1)} %bitcast.26), channel_id=1, replica_groups=mesh['far'=8,'pair'=2,'y'=4,'x'=4,'core'=2] {'far'}, dimensions={0} | all-to-all | bytes 204800 | tf_op jit(solution)/shard_map/all_to_all | solution.py:354
  78.2 0.2 hand_kernel.2
  78.4 8.2 %all_to_all.54.in_ref = f32[8,48,128]{2,1,0:T(8,128)S(1)} all-to-all(f32[8,48,128]{2,1,0:T(8,128)S(1)} %hand_kernel.2), channel_id=1, replica_groups=mesh['far'=8,'pair'=2,'y'=4,'x'=4,'core'=2] {'pair','y'}, dimensions={0} | all-to-all | bytes 393216 | tf_op jit(solution)/shard_map/all_to_all | solution.py:354
  86.6 0.6 second_gradient_kernel.1
  87.2 12.3 %all_to_all.55 = f32[8,25,1,128]{3,2,1,0:T(1,128)S(1)} all-to-all(f32[8,25,1,128]{3,2,1,0:T(1,128)S(1)} %bitcast.25), channel_id=1, replica_groups=mesh['far'=8,'pair'=2,'y'=4,'x'=4,'core'=2] {'x','core'}, dimensions={0} | all-to-all | bytes 204800 | tf_op jit(solution)/shard_map/all_to_all | solution.py:354
  99.5 0.6 second_image_kernel.1
  100.1 15.1 %all_to_all.56 = f32[8,25,1,128]{3,2,1,0:T(1,128)S(1)} all-to-all(f32[8,25,1,128]{3,2,1,0:T(1,128)S(1)} %bitcast.27), channel_id=1, replica_groups=mesh['far'=8,'pair'=2,'y'=4,'x'=4,'core'=2] {'far'}, dimensions={0} | all-to-all | bytes 204800 | tf_op jit(solution)/shard_map/all_to_all | solution.py:354
  115.2 0.2 hand_kernel.3
  115.4 8.2 %all_to_all.57.in_ref = f32[8,48,128]{2,1,0:T(8,128)S(1)} all-to-all(f32[8,48,128]{2,1,0:T(8,128)S(1)} %hand_kernel.3), channel_id=1, replica_groups=mesh['far'=8,'pair'=2,'y'=4,'x'=4,'core'=2] {'pair','y'}, dimensions={0} | all-to-all | bytes 393216 | tf_op jit(solution)/shard_map/all_to_all | solution.py:354
  123.5 0.6 third_gradient_kernel.1
  124.1 11.5 %all_to_all.58 = f32[8,25,1,128]{3,2,1,0:T(1,128)S(1)} all-to-all(f32[8,25,1,128]{3,2,1,0:T(1,128)S(1)} %bitcast.23), channel_id=1, replica_groups=mesh['far'=8,'pair'=2,'y'=4,'x'=4,'core'=2] {'x','core'}, dimensions={0} | all-to-all | bytes 204800 | tf_op jit(solution)/shard_map/all_to_all | solution.py:354
  135.6 0.3 third_image_kernel.1
  135.9 17.4 %all_to_all.59 = f32[64,1,1,128]{3,2,1,0:T(1,128)S(1)} all-to-all(f32[64,1,1,128]{3,2,1,0:T(1,128)S(1)} %bitcast.28), channel_id=1, replica_groups=mesh['far'=8,'pair'=2,'y'=4,'x'=4,'core'=2] {'far','pair','y'}, dimensions={0} | all-to-all | bytes 65536 | tf_op jit(solution)/shard_map/all_to_all | solution.py:354
  153.3 0.8 last_kernel.1
Async XLA Ops:
  3.8 42.2 %copy-start = (f32[24,128,128]{2,1,0:T(8,128)S(1)}, f32[24,128,128]{2,1,0:T(8,128)}, u32[]{:S(2)}) copy-start(f32[24,128,128]{2,1,0:T(8,128)} %tiles_ref.1) | copy-start | bytes 4718596
  3.8 42.2 %copy-start.2 = (f32[56,128]{1,0:T(8,128)S(1)}, f32[56,128]{1,0:T(8,128)}, u32[]{:S(2)}) copy-start(f32[56,128]{1,0:T(8,128)} %get-tuple-element.22.info_ref) | copy-start | bytes 86020
  46.0 15.2 %copy-start.1 = (f32[256,128]{1,0:T(8,128)S(1)}, f32[256,128]{1,0:T(8,128)}, u32[]{:S(2)}) copy-start(f32[256,128]{1,0:T(8,128)} %scores_ref.5) | copy-start | bytes 393220

commit v5 on v4

--- a/solution.py
+++ b/solution.py
@@ -5,13 +5,12 @@
 from jax import lax
 from jax.experimental import pallas as pl
 from jax.experimental.pallas import tpu as pltpu
-from jax.sharding import Mesh, PartitionSpec as P
-
-
-FAR, PAIR, Y, X, CORE = 8, 2, 4, 4, 2
-NEAR = PAIR * Y
-COLS = X * CORE
+from jax.sharding import PartitionSpec as P
+
+
+FAR, NEAR, COLS = 8, 8, 8
 ROWS = FAR * NEAR
+LEAD = 4
 CAP = 24
 TB = 128
 ROW_BLOCKS = 256
@@ -26,6 +25,11 @@
 INFO = 2 * CAP + EXTRA
 F32 = jnp.float32
 BF16 = jnp.bfloat16
+
+
+def places():
+    row = lax.axis_index("rows")
+    return lax.div(row, NEAR), lax.rem(row, NEAR)
 
 
 def iota(shape, dim):
@@ -167,13 +171,14 @@
         copy.wait()
     live = live_ref[0]
     pick_rows(scores, row_ref, picked)
-    row = index_row(col_ref, live, lax.axis_index("far") * MSG)
+    far, _ = places()
+    row = index_row(col_ref, live, lax.rem(far + FAR - LEAD, FAR) * MSG)
     sub = iota((CAP, TB), 0)
     mask = jnp.where(sub < live, 1.0, 0.0)
     own = jnp.full((CAP, TB), -1.0, F32)
     for j in range(CAP):
         own = jnp.where(sub == j, jnp.where(j < live, row_ref[j] + 1, -1).astype(F32), own)
-    place = lax.axis_index("x") * CORE + lax.axis_index("core")
+    place = lax.axis_index("cols")
     info_ref[:CAP, :] = mask
     info_ref[CAP : 2 * CAP, :] = own
     info_ref[2 * CAP :, :] = stack_rows([index_row(row_ref, live, place * MSG)])
@@ -199,8 +204,8 @@
     info_ref, in_ref, tiles_ref, out_ref, gradient_ref, hits_ref, split_ref
 ):
     split_tiles(tiles_ref, split_ref, 0, CAP)
-    far = lax.axis_index("far")
-    near = lax.axis_index("pair") * Y + lax.axis_index("y")
+    far, near = places()
+    slot = lax.rem(far + FAR - LEAD, FAR)
     lines = -(-LINE // TB)
     index = [[in_ref[i, LINE + k : LINE + k + 1, :] for k in range(lines)] for i in range(NEAR)]
     own_rows = index[0]
@@ -211,7 +216,7 @@
     for i in range(NEAR):
         found = jnp.zeros((CAP, TB), F32)
         for k in range(lines):
-            found = jnp.where(lane + k * TB == sub + far * MSG, index[i][k], found)
+            found = jnp.where(lane + k * TB == sub + slot * MSG, index[i][k], found)
         tile_part = jnp.sum(found, axis=1, keepdims=True)
         tile_part = jnp.where(tile_part == 0.0, -1.0, tile_part)
         share_part = ((far * NEAR + i) * SHARE + 1 + iota((SHARE, 1), 0)).astype(F32)
@@ -347,17 +352,26 @@
     )(*args)
 
 
-def swap(x, axes, count):
+FAR_ORDER = [(LEAD + i) % FAR for i in range(FAR)]
+GROUPS = {
+    "far": [[far * NEAR + near for far in FAR_ORDER] for near in range(NEAR)],
+    "near": [[far * NEAR + near for near in range(NEAR)] for far in range(FAR)],
+    "rows": [[far * NEAR + near for far in FAR_ORDER for near in range(NEAR)]],
+    "cols": None,
+}
+
+
+def swap(x, kind, count):
     shape = x.shape
     if len(shape) == 2:
         x = x.reshape(count, shape[0] // count, 1, TB)
-    return lax.all_to_all(x, axes, 0, 0, tiled=True).reshape(shape)
+    axis, groups = "cols" if kind == "cols" else "rows", GROUPS[kind]
+    return lax.all_to_all(x, axis, 0, 0, axis_index_groups=groups, tiled=True).reshape(shape)
 
 
 def local(tiles, tile_row, tile_col, tile_counts, scores):
     f = lambda *shape: (shape, F32)
     b = lambda *shape: (shape, BF16)
-    near, cols = ("pair", "y"), ("x", "core")
     to_far, to_near = f(LINE, TB), f(NEAR, HAND, TB)
     to_cols = f(SIDE, TB)
     image_shape, state_shape = f(ROW_BLOCKS, TB), f(EXTRA, TB)
@@ -383,51 +397,49 @@
     message, first, hand_hits, split = call(
         gathered_kernel,
         [to_cols, f(WANT, TB), b(NEAR * WANT, LINE), b(CAP, 2 * TB, TB)],
-        [info, swap(message, near, NEAR), tiles],
+        [info, swap(message, "near", NEAR), tiles],
     )
     message, image, row_hits = call(
         first_image_kernel,
         [to_far, image_shape, b(ROW_BLOCKS + CAP, SIDE)],
-        [info, swap(message, cols, COLS), split, scores],
+        [info, swap(message, "cols", COLS), split, scores],
     )
     (message,) = call(hand_kernel, [to_near], [swap(message, "far", FAR), hand_hits])
     message, product, second, state = call(
         second_gradient_kernel,
         [to_cols, f(WANT, TB), f(WANT, TB), state_shape],
-        [info, swap(message, near, NEAR), split, first],
+        [info, swap(message, "near", NEAR), split, first],
     )
     message, second_image = call(
         second_image_kernel,
         [to_far, image_shape],
-        [info, swap(message, cols, COLS), split, row_hits, scores, image, state],
+        [info, swap(message, "cols", COLS), split, row_hits, scores, image, state],
     )
     (message,) = call(hand_kernel, [to_near], [swap(message, "far", FAR), hand_hits])
     message, keep, later = call(
         third_gradient_kernel,
         [to_cols, f(3, SHARE, TB), state_shape],
-        [info, swap(message, near, NEAR), split, first, second, product, state],
+        [info, swap(message, "near", NEAR), split, first, second, product, state],
     )
     message, images = call(
         third_image_kernel,
         [f(ROWS, TB), f(3, ROW_BLOCKS, TB)],
-        [swap(message, cols, COLS), row_hits, scores, image, second_image, state, later],
+        [swap(message, "cols", COLS), row_hits, scores, image, second_image, state, later],
     )
     weights, residual = call(
         last_kernel,
         [f(SHARE, TB), image_shape],
-        [swap(message, ("far", *near), ROWS), keep, images, later],
+        [swap(message, "rows", ROWS), keep, images, later],
     )
     return weights, residual
 
 
 def solution(mesh):
-    rows, cols = ("far", "pair", "y"), ("x", "core")
-    every = rows + cols
-    fine = Mesh(mesh.devices.reshape(FAR, PAIR, Y, X, CORE), every)
+    every = ("rows", "cols")
     return jax.shard_map(
         local,
-        mesh=fine,
-        in_specs=(P(every, None, None), P(every), P(every), P(every), P(rows, None)),
-        out_specs=(P(cols + rows, None), P(rows, None)),
+        mesh=mesh,
+        in_specs=(P(every, None, None), P(every), P(every), P(every), P("rows", None)),
+        out_specs=(P(("cols", "rows"), None), P("rows", None)),
         check_vma=False,
     )

time: 155 us -> 148 us (0.955)
  blocking collectives: 145 us -> 138 us
    all_to_all x10, blocking collectives: 145 us -> 138 us  [swap(): lax.all_to_all(x, axis, 0, 0, axis_index_groups=groups, tiled=True)]
where the time goes in v5:
time: 148 us; the launch traced here: 147 us
  blocking collectives  138 us (93%)
  Pallas kernels  7.33 us (5%)
    all_to_all x10, blocking collectives, swap(): lax.all_to_all(x, axis, 0, 0, axis_index_groups=groups, tiled=True)  138 us
    pallas_call x11, Pallas kernels, call(): pl.pallas_call(kernel, out_shape=[jax.ShapeDtypeStruct(s, d) for s, d in...  7.33 us

profile of v5, /device:TPU:1, one launch (start us, length us, event | category | flops | bytes accessed | tf_op | source)
XLA Modules:
  0.0 147.1 jit_solution(5524506859809140161)
XLA Ops:
  1.3 2.5 %first_kernel.1 = (f32[200,128]{1,0:T(8,128)}, f32[56,128]{1,0:T(8,128)}) custom-call(s32[24]{0:T(128)} %row_hbm.1, s32[24]{0:T(128)} %col_hbm.1, s32[1]{0:T(128)S(6)} %copy.14.live_hbm, f32[24,128,128]{2,1,0:T(8,128)} %tiles_ref.1, f32[256,128]{1,0:T(8,128)} %scores_ref.5), custom_call_target="tpu_custom_call" | custom-call | tf_op jit(solution)/shard_map/first_kernel/pallas_call | solution.py:344
  3.8 0.0 copy-start
  3.8 0.0 copy-start.2
  3.8 23.5 %all_to_all.50 = f32[8,25,1,128]{3,2,1,0:T(1,128)S(1)} all-to-all(f32[8,25,1,128]{3,2,1,0:T(1,128)} %bitcast.29), channel_id=1, replica_groups={{256,320,384,448,0,64,128,192},{264,328,392,456,8,72,136,200},{272,336,..., dimensions={0} | all-to-all | bytes 204800 | tf_op jit(solution)/shard_map/all_to_all | solution.py:369
  27.3 0.1 relay_kernel.1
  27.4 15.8 %all_to_all.51.in_ref = f32[8,208,128]{2,1,0:T(8,128)S(1)} all-to-all(f32[8,208,128]{2,1,0:T(8,128)S(1)} %relay_kernel.1), channel_id=1, replica_groups={{0,8,16,24,32,40,48,56},{64,72,80,88,96,104,112,120},{128,136,144,152,1..., dimensions={0} | all-to-all | bytes 1703936 | tf_op jit(solution)/shard_map/all_to_all | solution.py:369
  43.1 0.0 copy-start.1
  43.1 0.0 copy-done
  43.1 0.0 copy-done.2
  43.1 0.9 gathered_kernel.1
  44.0 12.2 %all_to_all.52 = f32[8,25,1,128]{3,2,1,0:T(1,128)S(1)} all-to-all(f32[8,25,1,128]{3,2,1,0:T(1,128)S(1)} %bitcast.24), channel_id=1, replica_groups=mesh['rows'=64,'cols'=8] {'cols'}, dimensions={0} | all-to-all | bytes 204800 | tf_op jit(solution)/shard_map/all_to_all | solution.py:369
  56.3 0.0 copy-done.1
  56.3 0.6 first_image_kernel.1
  56.9 17.0 %all_to_all.53 = f32[8,25,1,128]{3,2,1,0:T(1,128)S(1)} all-to-all(f32[8,25,1,128]{3,2,1,0:T(1,128)S(1)} %bitcast.26), channel_id=1, replica_groups={{256,320,384,448,0,64,128,192},{264,328,392,456,8,72,136,200},{272,336,..., dimensions={0} | all-to-all | bytes 204800 | tf_op jit(solution)/shard_map/all_to_all | solution.py:369
  73.9 0.2 hand_kernel.2
  74.1 8.2 %all_to_all.54.in_ref = f32[8,48,128]{2,1,0:T(8,128)S(1)} all-to-all(f32[8,48,128]{2,1,0:T(8,128)S(1)} %hand_kernel.2), channel_id=1, replica_groups={{0,8,16,24,32,40,48,56},{64,72,80,88,96,104,112,120},{128,136,144,152,1..., dimensions={0} | all-to-all | bytes 393216 | tf_op jit(solution)/shard_map/all_to_all | solution.py:369
  82.3 0.6 second_gradient_kernel.1
  83.0 9.9 %all_to_all.55 = f32[8,25,1,128]{3,2,1,0:T(1,128)S(1)} all-to-all(f32[8,25,1,128]{3,2,1,0:T(1,128)S(1)} %bitcast.25), channel_id=1, replica_groups=mesh['rows'=64,'cols'=8] {'cols'}, dimensions={0} | all-to-all | bytes 204800 | tf_op jit(solution)/shard_map/all_to_all | solution.py:369
  92.8 0.6 second_image_kernel.1
  93.4 17.7 %all_to_all.56 = f32[8,25,1,128]{3,2,1,0:T(1,128)S(1)} all-to-all(f32[8,25,1,128]{3,2,1,0:T(1,128)S(1)} %bitcast.27), channel_id=1, replica_groups={{256,320,384,448,0,64,128,192},{264,328,392,456,8,72,136,200},{272,336,..., dimensions={0} | all-to-all | bytes 204800 | tf_op jit(solution)/shard_map/all_to_all | solution.py:369
  111.1 0.2 hand_kernel.3
  111.3 8.2 %all_to_all.57.in_ref = f32[8,48,128]{2,1,0:T(8,128)S(1)} all-to-all(f32[8,48,128]{2,1,0:T(8,128)S(1)} %hand_kernel.3), channel_id=1, replica_groups={{0,8,16,24,32,40,48,56},{64,72,80,88,96,104,112,120},{128,136,144,152,1..., dimensions={0} | all-to-all | bytes 393216 | tf_op jit(solution)/shard_map/all_to_all | solution.py:369
  119.5 0.6 third_gradient_kernel.1
  120.1 9.5 %all_to_all.58 = f32[8,25,1,128]{3,2,1,0:T(1,128)S(1)} all-to-all(f32[8,25,1,128]{3,2,1,0:T(1,128)S(1)} %bitcast.23), channel_id=1, replica_groups=mesh['rows'=64,'cols'=8] {'cols'}, dimensions={0} | all-to-all | bytes 204800 | tf_op jit(solution)/shard_map/all_to_all | solution.py:369
  129.6 0.3 third_image_kernel.1
  129.9 16.5 %all_to_all.59 = f32[64,1,1,128]{3,2,1,0:T(1,128)S(1)} all-to-all(f32[64,1,1,128]{3,2,1,0:T(1,128)S(1)} %bitcast.28), channel_id=1, replica_groups={{256,264,272,280,288,296,304,312,320,328,336,344,352,360,368,376,384,39..., dimensions={0} | all-to-all | bytes 65536 | tf_op jit(solution)/shard_map/all_to_all | solution.py:369
  146.4 0.8 last_kernel.1
Async XLA Ops:
  3.8 39.3 %copy-start = (f32[24,128,128]{2,1,0:T(8,128)S(1)}, f32[24,128,128]{2,1,0:T(8,128)}, u32[]{:S(2)}) copy-start(f32[24,128,128]{2,1,0:T(8,128)} %tiles_ref.1) | copy-start | bytes 4718596
  3.8 39.3 %copy-start.2 = (f32[56,128]{1,0:T(8,128)S(1)}, f32[56,128]{1,0:T(8,128)}, u32[]{:S(2)}) copy-start(f32[56,128]{1,0:T(8,128)} %get-tuple-element.22.info_ref) | copy-start | bytes 86020
  43.1 13.2 %copy-start.1 = (f32[256,128]{1,0:T(8,128)S(1)}, f32[256,128]{1,0:T(8,128)}, u32[]{:S(2)}) copy-start(f32[256,128]{1,0:T(8,128)} %scores_ref.5) | copy-start | bytes 393220

commit v6 on v5

--- a/solution.py
+++ b/solution.py
@@ -10,7 +10,9 @@
 
 FAR, NEAR, COLS = 8, 8, 8
 ROWS = FAR * NEAR
-LEAD = 4
+FAR_ORDER = [4, 0, 1, 7, 2, 6, 3, 5]
+NEAR_ORDER = [2, 3, 4, 5, 6, 7, 0, 1]
+COL_ORDER = [5, 1, 7, 3, 4, 0, 6, 2]
 CAP = 24
 TB = 128
 ROW_BLOCKS = 256
@@ -30,6 +32,13 @@
 def places():
     row = lax.axis_index("rows")
     return lax.div(row, NEAR), lax.rem(row, NEAR)
+
+
+def slot_of(place, order):
+    slot = 0
+    for i, member in enumerate(order):
+        slot = jnp.where(place == member, i, slot)
+    return slot
 
 
 def iota(shape, dim):
@@ -172,13 +181,13 @@
     live = live_ref[0]
     pick_rows(scores, row_ref, picked)
     far, _ = places()
-    row = index_row(col_ref, live, lax.rem(far + FAR - LEAD, FAR) * MSG)
+    row = index_row(col_ref, live, slot_of(far, FAR_ORDER) * MSG)
     sub = iota((CAP, TB), 0)
     mask = jnp.where(sub < live, 1.0, 0.0)
     own = jnp.full((CAP, TB), -1.0, F32)
     for j in range(CAP):
         own = jnp.where(sub == j, jnp.where(j < live, row_ref[j] + 1, -1).astype(F32), own)
-    place = lax.axis_index("cols")
+    place = slot_of(lax.axis_index("cols"), COL_ORDER)
     info_ref[:CAP, :] = mask
     info_ref[CAP : 2 * CAP, :] = own
     info_ref[2 * CAP :, :] = stack_rows([index_row(row_ref, live, place * MSG)])
@@ -205,12 +214,12 @@
 ):
     split_tiles(tiles_ref, split_ref, 0, CAP)
     far, near = places()
-    slot = lax.rem(far + FAR - LEAD, FAR)
+    slot = slot_of(far, FAR_ORDER)
     lines = -(-LINE // TB)
     index = [[in_ref[i, LINE + k : LINE + k + 1, :] for k in range(lines)] for i in range(NEAR)]
     own_rows = index[0]
     for i in range(1, NEAR):
-        own_rows = [jnp.where(near == i, new, old) for new, old in zip(index[i], own_rows)]
+        own_rows = [jnp.where(near == NEAR_ORDER[i], new, old) for new, old in zip(index[i], own_rows)]
     own_wanted = jnp.zeros((WANT, 1), F32)
     lane, sub = iota((CAP, TB), 1), iota((CAP, TB), 0)
     for i in range(NEAR):
@@ -219,10 +228,10 @@
             found = jnp.where(lane + k * TB == sub + slot * MSG, index[i][k], found)
         tile_part = jnp.sum(found, axis=1, keepdims=True)
         tile_part = jnp.where(tile_part == 0.0, -1.0, tile_part)
-        share_part = ((far * NEAR + i) * SHARE + 1 + iota((SHARE, 1), 0)).astype(F32)
+        share_part = ((far * NEAR + NEAR_ORDER[i]) * SHARE + 1 + iota((SHARE, 1), 0)).astype(F32)
         wanted = jnp.concatenate([tile_part, share_part], axis=0)
         hits_ref[WANT * i : WANT * (i + 1), :] = hits_of(wanted, own_rows, LINE)
-        own_wanted = jnp.where(near == i, wanted, own_wanted)
+        own_wanted = jnp.where(near == NEAR_ORDER[i], wanted, own_wanted)
     gradient = jnp.zeros((WANT, TB), F32)
     for i in range(NEAR):
         gradient += picked_sum(hits_of(own_wanted, index[i], LINE), in_ref[i, :LINE, :])
@@ -352,12 +361,11 @@
     )(*args)
 
 
-FAR_ORDER = [(LEAD + i) % FAR for i in range(FAR)]
 GROUPS = {
     "far": [[far * NEAR + near for far in FAR_ORDER] for near in range(NEAR)],
-    "near": [[far * NEAR + near for near in range(NEAR)] for far in range(FAR)],
-    "rows": [[far * NEAR + near for far in FAR_ORDER for near in range(NEAR)]],
-    "cols": None,
+    "near": [[far * NEAR + near for near in NEAR_ORDER] for far in range(FAR)],
+    "rows": [[far * NEAR + near for far in FAR_ORDER for near in NEAR_ORDER]],
+    "cols": [COL_ORDER],
 }
 
 

time: 148 us -> 142 us (0.959)
  blocking collectives: 138 us -> 132 us
    all_to_all x10, blocking collectives: 138 us -> 132 us  [swap(): lax.all_to_all(x, axis, 0, 0, axis_index_groups=groups, tiled=True)]
where the time goes in v6:
time: 142 us; the launch traced here: 141 us
  blocking collectives  132 us (93%)
  Pallas kernels  7.32 us (5%)
    all_to_all x10, blocking collectives, swap(): lax.all_to_all(x, axis, 0, 0, axis_index_groups=groups, tiled=True)  132 us
    pallas_call x11, Pallas kernels, call(): pl.pallas_call(kernel, out_shape=[jax.ShapeDtypeStruct(s, d) for s, d in...  7.32 us

profile of v6, /device:TPU:1, one launch (start us, length us, event | category | flops | bytes accessed | tf_op | source)
XLA Modules:
  0.0 140.9 jit_solution(3365661980282298531)
XLA Ops:
  1.3 2.5 %first_kernel.1 = (f32[200,128]{1,0:T(8,128)}, f32[56,128]{1,0:T(8,128)}) custom-call(s32[24]{0:T(128)} %row_hbm.1, s32[24]{0:T(128)} %col_hbm.1, s32[1]{0:T(128)S(6)} %copy.14.live_hbm, f32[24,128,128]{2,1,0:T(8,128)} %tiles_ref.1, f32[256,128]{1,0:T(8,128)} %scores_ref.5), custom_call_target="tpu_custom_call" | custom-call | tf_op jit(solution)/shard_map/first_kernel/pallas_call | solution.py:353
  3.8 0.0 copy-start
  3.8 0.0 copy-start.2
  3.8 23.5 %all_to_all.50 = f32[8,25,1,128]{3,2,1,0:T(1,128)S(1)} all-to-all(f32[8,25,1,128]{3,2,1,0:T(1,128)} %bitcast.29), channel_id=1, replica_groups={{256,0,64,448,128,384,192,320},{264,8,72,456,136,392,200,328},{272,16,8..., dimensions={0} | all-to-all | bytes 204800 | tf_op jit(solution)/shard_map/all_to_all | solution.py:377
  27.3 0.1 relay_kernel.1
  27.3 14.5 %all_to_all.51.in_ref = f32[8,208,128]{2,1,0:T(8,128)S(1)} all-to-all(f32[8,208,128]{2,1,0:T(8,128)S(1)} %relay_kernel.1), channel_id=1, replica_groups={{16,24,32,40,48,56,0,8},{80,88,96,104,112,120,64,72},{144,152,160,168,1..., dimensions={0} | all-to-all | bytes 1703936 | tf_op jit(solution)/shard_map/all_to_all | solution.py:377
  41.9 0.0 copy-start.1
  41.9 0.0 copy-done
  41.9 0.0 copy-done.2
  41.9 0.9 gathered_kernel.1
  42.8 10.3 %all_to_all.52 = f32[8,25,1,128]{3,2,1,0:T(1,128)S(1)} all-to-all(f32[8,25,1,128]{3,2,1,0:T(1,128)S(1)} %bitcast.24), channel_id=1, replica_groups={{5,1,7,3,4,0,6,2},{13,9,15,11,12,8,14,10},{21,17,23,19,20,16,22,18},{29..., dimensions={0} | all-to-all | bytes 204800 | tf_op jit(solution)/shard_map/all_to_all | solution.py:377
  53.1 0.0 copy-done.1
  53.1 0.6 first_image_kernel.1
  53.7 16.9 %all_to_all.53 = f32[8,25,1,128]{3,2,1,0:T(1,128)S(1)} all-to-all(f32[8,25,1,128]{3,2,1,0:T(1,128)S(1)} %bitcast.26), channel_id=1, replica_groups={{256,0,64,448,128,384,192,320},{264,8,72,456,136,392,200,328},{272,16,8..., dimensions={0} | all-to-all | bytes 204800 | tf_op jit(solution)/shard_map/all_to_all | solution.py:377
  70.6 0.2 hand_kernel.2
  70.8 8.6 %all_to_all.54.in_ref = f32[8,48,128]{2,1,0:T(8,128)S(1)} all-to-all(f32[8,48,128]{2,1,0:T(8,128)S(1)} %hand_kernel.2), channel_id=1, replica_groups={{16,24,32,40,48,56,0,8},{80,88,96,104,112,120,64,72},{144,152,160,168,1..., dimensions={0} | all-to-all | bytes 393216 | tf_op jit(solution)/shard_map/all_to_all | solution.py:377
  79.4 0.6 second_gradient_kernel.1
  80.0 8.5 %all_to_all.55 = f32[8,25,1,128]{3,2,1,0:T(1,128)S(1)} all-to-all(f32[8,25,1,128]{3,2,1,0:T(1,128)S(1)} %bitcast.25), channel_id=1, replica_groups={{5,1,7,3,4,0,6,2},{13,9,15,11,12,8,14,10},{21,17,23,19,20,16,22,18},{29..., dimensions={0} | all-to-all | bytes 204800 | tf_op jit(solution)/shard_map/all_to_all | solution.py:377
  88.5 0.6 second_image_kernel.1
  89.0 16.6 %all_to_all.56 = f32[8,25,1,128]{3,2,1,0:T(1,128)S(1)} all-to-all(f32[8,25,1,128]{3,2,1,0:T(1,128)S(1)} %bitcast.27), channel_id=1, replica_groups={{256,0,64,448,128,384,192,320},{264,8,72,456,136,392,200,328},{272,16,8..., dimensions={0} | all-to-all | bytes 204800 | tf_op jit(solution)/shard_map/all_to_all | solution.py:377
  105.6 0.2 hand_kernel.3
  105.8 8.0 %all_to_all.57.in_ref = f32[8,48,128]{2,1,0:T(8,128)S(1)} all-to-all(f32[8,48,128]{2,1,0:T(8,128)S(1)} %hand_kernel.3), channel_id=1, replica_groups={{16,24,32,40,48,56,0,8},{80,88,96,104,112,120,64,72},{144,152,160,168,1..., dimensions={0} | all-to-all | bytes 393216 | tf_op jit(solution)/shard_map/all_to_all | solution.py:377
  113.8 0.6 third_gradient_kernel.1
  114.4 8.9 %all_to_all.58 = f32[8,25,1,128]{3,2,1,0:T(1,128)S(1)} all-to-all(f32[8,25,1,128]{3,2,1,0:T(1,128)S(1)} %bitcast.23), channel_id=1, replica_groups={{5,1,7,3,4,0,6,2},{13,9,15,11,12,8,14,10},{21,17,23,19,20,16,22,18},{29..., dimensions={0} | all-to-all | bytes 204800 | tf_op jit(solution)/shard_map/all_to_all | solution.py:377
  123.4 0.3 third_image_kernel.1
  123.7 16.4 %all_to_all.59 = f32[64,1,1,128]{3,2,1,0:T(1,128)S(1)} all-to-all(f32[64,1,1,128]{3,2,1,0:T(1,128)S(1)} %bitcast.28), channel_id=1, replica_groups={{272,280,288,296,304,312,256,264,16,24,32,40,48,56,0,8,80,88,96,104,112..., dimensions={0} | all-to-all | bytes 65536 | tf_op jit(solution)/shard_map/all_to_all | solution.py:377
  140.1 0.8 last_kernel.1
Async XLA Ops:
  3.8 38.1 %copy-start = (f32[24,128,128]{2,1,0:T(8,128)S(1)}, f32[24,128,128]{2,1,0:T(8,128)}, u32[]{:S(2)}) copy-start(f32[24,128,128]{2,1,0:T(8,128)} %tiles_ref.1) | copy-start | bytes 4718596
  3.8 38.0 %copy-start.2 = (f32[56,128]{1,0:T(8,128)S(1)}, f32[56,128]{1,0:T(8,128)}, u32[]{:S(2)}) copy-start(f32[56,128]{1,0:T(8,128)} %get-tuple-element.22.info_ref) | copy-start | bytes 86020
  41.9 11.2 %copy-start.1 = (f32[256,128]{1,0:T(8,128)S(1)}, f32[256,128]{1,0:T(8,128)}, u32[]{:S(2)}) copy-start(f32[256,128]{1,0:T(8,128)} %scores_ref.5) | copy-start | bytes 393220

commit v7 on v6

--- a/solution.py
+++ b/solution.py
@@ -22,7 +22,7 @@
 MSG = CAP + 1
 LINE = FAR * MSG
 SIDE = COLS * MSG
-HAND = WANT + EXTRA
+HAND = WANT + 1
 PARTS = 3
 INFO = 2 * CAP + EXTRA
 F32 = jnp.float32
@@ -201,8 +201,9 @@
 def relay_kernel(in_ref, out_ref):
     rows = index_lanes(in_ref, FAR)
     for i in range(NEAR):
-        out_ref[i, :LINE, :] = in_ref[...]
-        out_ref[i, LINE:, :] = stack_rows(rows)
+        out_ref[i] = in_ref[...]
+        for k, row in enumerate(rows):
+            out_ref[i, MSG * k + CAP : MSG * (k + 1), :] = row
 
 
 def send_forward(vectors, split_ref, info_ref, row, out_ref):
@@ -216,11 +217,14 @@
     far, near = places()
     slot = slot_of(far, FAR_ORDER)
     lines = -(-LINE // TB)
-    index = [[in_ref[i, LINE + k : LINE + k + 1, :] for k in range(lines)] for i in range(NEAR)]
+    index = [
+        [in_ref[i, MSG * k + CAP : MSG * (k + 1), :] for k in range(lines)] for i in range(NEAR)
+    ]
     own_rows = index[0]
     for i in range(1, NEAR):
         own_rows = [jnp.where(near == NEAR_ORDER[i], new, old) for new, old in zip(index[i], own_rows)]
     own_wanted = jnp.zeros((WANT, 1), F32)
+    every_wanted = []
     lane, sub = iota((CAP, TB), 1), iota((CAP, TB), 0)
     for i in range(NEAR):
         found = jnp.zeros((CAP, TB), F32)
@@ -230,11 +234,12 @@
         tile_part = jnp.where(tile_part == 0.0, -1.0, tile_part)
         share_part = ((far * NEAR + NEAR_ORDER[i]) * SHARE + 1 + iota((SHARE, 1), 0)).astype(F32)
         wanted = jnp.concatenate([tile_part, share_part], axis=0)
-        hits_ref[WANT * i : WANT * (i + 1), :] = hits_of(wanted, own_rows, LINE)
+        every_wanted.append(wanted)
         own_wanted = jnp.where(near == NEAR_ORDER[i], wanted, own_wanted)
+    hits_ref[...] = hits_of(jnp.concatenate(every_wanted, axis=0), own_rows, LINE)
     gradient = jnp.zeros((WANT, TB), F32)
     for i in range(NEAR):
-        gradient += picked_sum(hits_of(own_wanted, index[i], LINE), in_ref[i, :LINE, :])
+        gradient += picked_sum(hits_of(own_wanted, index[i], LINE), in_ref[i])
     gradient_ref[...] = gradient
     send_forward(gradient[:CAP], split_ref, info_ref, info_ref[2 * CAP : 2 * CAP + 1, :], out_ref)
 
@@ -259,17 +264,17 @@
 
 
 def hand_kernel(in_ref, hits_ref, out_ref):
-    extra = jnp.broadcast_to(extra_sum(in_ref, FAR), (EXTRA, TB))
+    extra = extra_sum(in_ref, FAR)
     sums = picked_sum(hits_ref[...], in_ref[...])
     for i in range(NEAR):
-        out_ref[i, :WANT, :] = sums[WANT * i : WANT * (i + 1)]
-        out_ref[i, WANT:, :] = extra
+        some = jnp.concatenate([sums[WANT * i : WANT * (i + 1)], extra], axis=0)
+        out_ref[HAND * i : HAND * (i + 1), :] = some
 
 
 def added(in_ref):
-    total = in_ref[0]
-    for i in range(1, in_ref.shape[0]):
-        total = total + in_ref[i]
+    total = in_ref[:HAND, :]
+    for i in range(1, NEAR):
+        total = total + in_ref[HAND * i : HAND * (i + 1), :]
     return total
 
 
@@ -380,7 +385,7 @@
 def local(tiles, tile_row, tile_col, tile_counts, scores):
     f = lambda *shape: (shape, F32)
     b = lambda *shape: (shape, BF16)
-    to_far, to_near = f(LINE, TB), f(NEAR, HAND, TB)
+    to_far, to_near = f(LINE, TB), f(NEAR * HAND, TB)
     to_cols = f(SIDE, TB)
     image_shape, state_shape = f(ROW_BLOCKS, TB), f(EXTRA, TB)
 
@@ -401,7 +406,7 @@
         pltpu.HBM,
         62 * 2**20,
     )
-    (message,) = call(relay_kernel, [f(NEAR, LINE + EXTRA, TB)], [swap(message, "far", FAR)])
+    (message,) = call(relay_kernel, [f(NEAR, LINE, TB)], [swap(message, "far", FAR)])
     message, first, hand_hits, split = call(
         gathered_kernel,
         [to_cols, f(WANT, TB), b(NEAR * WANT, LINE), b(CAP, 2 * TB, TB)],

time: 142 us -> 142 us (level)
  no operation moved by 1% of the time
where the time goes in v7:
time: 142 us; the launch traced here: 140 us
  blocking collectives  132 us (93%)
  Pallas kernels  7.32 us (5%)
    all_to_all x10, blocking collectives, swap(): lax.all_to_all(x, axis, 0, 0, axis_index_groups=groups, tiled=True)  132 us
    pallas_call x11, Pallas kernels, call(): pl.pallas_call(kernel, out_shape=[jax.ShapeDtypeStruct(s, d) for s, d in...  7.32 us

profile of v7, /device:TPU:1, one launch (start us, length us, event | category | flops | bytes accessed | tf_op | source)
XLA Modules:
  0.0 140.4 jit_solution(4590990268582239678)
XLA Ops:
  1.3 2.5 %first_kernel.1 = (f32[200,128]{1,0:T(8,128)}, f32[56,128]{1,0:T(8,128)}) custom-call(s32[24]{0:T(128)} %row_hbm.1, s32[24]{0:T(128)} %col_hbm.1, s32[1]{0:T(128)S(6)} %copy.16.live_hbm, f32[24,128,128]{2,1,0:T(8,128)} %tiles_ref.1, f32[256,128]{1,0:T(8,128)} %scores_ref.5), custom_call_target="tpu_custom_call" | custom-call | tf_op jit(solution)/shard_map/first_kernel/pallas_call | solution.py:358
  3.8 0.0 copy-start
  3.8 0.0 copy-start.2
  3.8 23.5 %all_to_all.50 = f32[8,25,1,128]{3,2,1,0:T(1,128)S(1)} all-to-all(f32[8,25,1,128]{3,2,1,0:T(1,128)} %bitcast.37), channel_id=1, replica_groups={{256,0,64,448,128,384,192,320},{264,8,72,456,136,392,200,328},{272,16,8..., dimensions={0} | all-to-all | bytes 204800 | tf_op jit(solution)/shard_map/all_to_all | solution.py:382
  27.3 0.1 relay_kernel.1
  27.3 14.2 %all_to_all.51.in_ref = f32[8,200,128]{2,1,0:T(8,128)S(1)} all-to-all(f32[8,200,128]{2,1,0:T(8,128)S(1)} %relay_kernel.1), channel_id=1, replica_groups={{16,24,32,40,48,56,0,8},{80,88,96,104,112,120,64,72},{144,152,160,168,1..., dimensions={0} | all-to-all | bytes 1638400 | tf_op jit(solution)/shard_map/all_to_all | solution.py:382
  41.5 0.0 copy-start.1
  41.5 0.0 copy-done
  41.5 0.0 copy-done.2
  41.5 0.9 gathered_kernel.1
  42.4 10.3 %all_to_all.52 = f32[8,25,1,128]{3,2,1,0:T(1,128)S(1)} all-to-all(f32[8,25,1,128]{3,2,1,0:T(1,128)S(1)} %bitcast.32), channel_id=1, replica_groups={{5,1,7,3,4,0,6,2},{13,9,15,11,12,8,14,10},{21,17,23,19,20,16,22,18},{29..., dimensions={0} | all-to-all | bytes 204800 | tf_op jit(solution)/shard_map/all_to_all | solution.py:382
  52.7 0.0 copy-done.1
  52.7 0.6 first_image_kernel.1
  53.4 16.9 %all_to_all.53 = f32[8,25,1,128]{3,2,1,0:T(1,128)S(1)} all-to-all(f32[8,25,1,128]{3,2,1,0:T(1,128)S(1)} %bitcast.34), channel_id=1, replica_groups={{256,0,64,448,128,384,192,320},{264,8,72,456,136,392,200,328},{272,16,8..., dimensions={0} | all-to-all | bytes 204800 | tf_op jit(solution)/shard_map/all_to_all | solution.py:382
  70.3 0.2 hand_kernel.2
  70.5 8.5 %all_to_all.54 = f32[8,41,1,128]{3,2,1,0:T(1,128)S(1)} all-to-all(f32[8,41,1,128]{3,2,1,0:T(1,128)S(1)} %bitcast.23), channel_id=1, replica_groups={{16,24,32,40,48,56,0,8},{80,88,96,104,112,120,64,72},{144,152,160,168,1..., dimensions={0} | all-to-all | bytes 335872 | tf_op jit(solution)/shard_map/all_to_all | solution.py:382
  79.0 0.6 second_gradient_kernel.1
  79.6 8.5 %all_to_all.55 = f32[8,25,1,128]{3,2,1,0:T(1,128)S(1)} all-to-all(f32[8,25,1,128]{3,2,1,0:T(1,128)S(1)} %bitcast.33), channel_id=1, replica_groups={{5,1,7,3,4,0,6,2},{13,9,15,11,12,8,14,10},{21,17,23,19,20,16,22,18},{29..., dimensions={0} | all-to-all | bytes 204800 | tf_op jit(solution)/shard_map/all_to_all | solution.py:382
  88.1 0.6 second_image_kernel.1
  88.6 16.5 %all_to_all.56 = f32[8,25,1,128]{3,2,1,0:T(1,128)S(1)} all-to-all(f32[8,25,1,128]{3,2,1,0:T(1,128)S(1)} %bitcast.35), channel_id=1, replica_groups={{256,0,64,448,128,384,192,320},{264,8,72,456,136,392,200,328},{272,16,8..., dimensions={0} | all-to-all | bytes 204800 | tf_op jit(solution)/shard_map/all_to_all | solution.py:382
  105.2 0.2 hand_kernel.3
  105.4 8.0 %all_to_all.57 = f32[8,41,1,128]{3,2,1,0:T(1,128)S(1)} all-to-all(f32[8,41,1,128]{3,2,1,0:T(1,128)S(1)} %bitcast.22), channel_id=1, replica_groups={{16,24,32,40,48,56,0,8},{80,88,96,104,112,120,64,72},{144,152,160,168,1..., dimensions={0} | all-to-all | bytes 335872 | tf_op jit(solution)/shard_map/all_to_all | solution.py:382
  113.4 0.6 third_gradient_kernel.1
  113.9 8.9 %all_to_all.58 = f32[8,25,1,128]{3,2,1,0:T(1,128)S(1)} all-to-all(f32[8,25,1,128]{3,2,1,0:T(1,128)S(1)} %bitcast.31), channel_id=1, replica_groups={{5,1,7,3,4,0,6,2},{13,9,15,11,12,8,14,10},{21,17,23,19,20,16,22,18},{29..., dimensions={0} | all-to-all | bytes 204800 | tf_op jit(solution)/shard_map/all_to_all | solution.py:382
  122.8 0.3 third_image_kernel.1
  123.1 16.5 %all_to_all.59 = f32[64,1,1,128]{3,2,1,0:T(1,128)S(1)} all-to-all(f32[64,1,1,128]{3,2,1,0:T(1,128)S(1)} %bitcast.36), channel_id=1, replica_groups={{272,280,288,296,304,312,256,264,16,24,32,40,48,56,0,8,80,88,96,104,112..., dimensions={0} | all-to-all | bytes 65536 | tf_op jit(solution)/shard_map/all_to_all | solution.py:382
  139.6 0.8 last_kernel.1
Async XLA Ops:
  3.8 37.7 %copy-start = (f32[24,128,128]{2,1,0:T(8,128)S(1)}, f32[24,128,128]{2,1,0:T(8,128)}, u32[]{:S(2)}) copy-start(f32[24,128,128]{2,1,0:T(8,128)} %tiles_ref.1) | copy-start | bytes 4718596
  3.8 37.7 %copy-start.2 = (f32[56,128]{1,0:T(8,128)S(1)}, f32[56,128]{1,0:T(8,128)}, u32[]{:S(2)}) copy-start(f32[56,128]{1,0:T(8,128)} %get-tuple-element.22.info_ref) | copy-start | bytes 86020
  41.5 11.2 %copy-start.1 = (f32[256,128]{1,0:T(8,128)S(1)}, f32[256,128]{1,0:T(8,128)}, u32[]{:S(2)}) copy-start(f32[256,128]{1,0:T(8,128)} %scores_ref.5) | copy-start | bytes 393220

commit v8 on v7

--- a/solution.py
+++ b/solution.py
@@ -10,7 +10,7 @@
 
 FAR, NEAR, COLS = 8, 8, 8
 ROWS = FAR * NEAR
-FAR_ORDER = [4, 0, 1, 7, 2, 6, 3, 5]
+FAR_ORDERS = [[4, 0, 1, 7, 2, 6, 3, 5], [4, 0, 7, 1, 6, 2, 5, 3]]
 NEAR_ORDER = [2, 3, 4, 5, 6, 7, 0, 1]
 COL_ORDER = [5, 1, 7, 3, 4, 0, 6, 2]
 CAP = 24
@@ -23,7 +23,7 @@
 LINE = FAR * MSG
 SIDE = COLS * MSG
 HAND = WANT + 1
-PARTS = 3
+PARTS = CAP // 8
 INFO = 2 * CAP + EXTRA
 F32 = jnp.float32
 BF16 = jnp.bfloat16
@@ -41,6 +41,11 @@
     return slot
 
 
+def far_slot(far):
+    first, second = [slot_of(far, order) for order in FAR_ORDERS]
+    return jnp.where(lax.rem(lax.axis_index("cols"), 2) == 0, first, second)
+
+
 def iota(shape, dim):
     return lax.broadcasted_iota(jnp.int32, shape, dim)
 
@@ -60,26 +65,26 @@
     return out[:, :TB] + out[:, TB:]
 
 
+def times_group(g, vectors, split_ref, live, transposed):
+    sub = iota((8, TB), 0)
+    high, low = two_parts(vectors[8 * g : 8 * g + 8])
+    both = jnp.concatenate([high, low], axis=0).astype(BF16)
+    if transposed:
+        both = jnp.concatenate([both, both], axis=1)
+    total = jnp.zeros((8, TB), F32)
+    for k in range(8):
+        tile = split_ref[8 * g + k]
+        if transposed:
+            out = jnp.dot(both, tile, preferred_element_type=F32)
+        else:
+            out = lax.dot_general(both, tile, (((1,), (1,)), ((), ())), preferred_element_type=F32)
+            out = out[:, :TB] + out[:, TB:]
+        total = jnp.where(sub == k, out[:8] + out[8:], total)
+    return jnp.where(live[8 * g : 8 * g + 8] > 0.0, total, 0.0)
+
+
 def times_tiles(vectors, split_ref, live, transposed):
-    sub = iota((8, TB), 0)
-    groups = []
-    for g in range(CAP // 8):
-        high, low = two_parts(vectors[8 * g : 8 * g + 8])
-        both = jnp.concatenate([high, low], axis=0).astype(BF16)
-        if transposed:
-            both = jnp.concatenate([both, both], axis=1)
-        total = jnp.zeros((8, TB), F32)
-        for k in range(8):
-            tile = split_ref[8 * g + k]
-            if transposed:
-                out = jnp.dot(both, tile, preferred_element_type=F32)
-            else:
-                out = lax.dot_general(
-                    both, tile, (((1,), (1,)), ((), ())), preferred_element_type=F32
-                )
-                out = out[:, :TB] + out[:, TB:]
-            total = jnp.where(sub == k, out[:8] + out[8:], total)
-        groups.append(jnp.where(live[8 * g : 8 * g + 8] > 0.0, total, 0.0))
+    groups = [times_group(g, vectors, split_ref, live, transposed) for g in range(CAP // 8)]
     return jnp.concatenate(groups, axis=0)
 
 
@@ -181,7 +186,7 @@
     live = live_ref[0]
     pick_rows(scores, row_ref, picked)
     far, _ = places()
-    row = index_row(col_ref, live, slot_of(far, FAR_ORDER) * MSG)
+    row = index_row(col_ref, live, far_slot(far) * MSG)
     sub = iota((CAP, TB), 0)
     mask = jnp.where(sub < live, 1.0, 0.0)
     own = jnp.full((CAP, TB), -1.0, F32)
@@ -191,10 +196,12 @@
     info_ref[:CAP, :] = mask
     info_ref[CAP : 2 * CAP, :] = own
     info_ref[2 * CAP :, :] = stack_rows([index_row(row_ref, live, place * MSG)])
+    groups, rows = [], picked[...]
     for i in range(PARTS):
         copies[4 + i].wait()
         split_tiles(tiles, split_ref, part * i, part * (i + 1))
-    sums = times_tiles(picked[...], split_ref, mask, True)
+        groups.append(times_group(i, rows, split_ref, mask, True))
+    sums = jnp.concatenate(groups, axis=0)
     send_to_all(out_ref, FAR, sums, row)
 
 
@@ -206,16 +213,16 @@
             out_ref[i, MSG * k + CAP : MSG * (k + 1), :] = row
 
 
-def send_forward(vectors, split_ref, info_ref, row, out_ref):
-    send_to_all(out_ref, COLS, times_tiles(vectors, split_ref, info_ref[:CAP, :], False), row)
+def forward(vectors, split_ref, info_ref):
+    return times_tiles(vectors[:CAP], split_ref, info_ref[:CAP, :], False)
 
 
 def gathered_kernel(
-    info_ref, in_ref, tiles_ref, out_ref, gradient_ref, hits_ref, split_ref
+    info_ref, in_ref, tiles_ref, out_ref, gradient_ref, hits_ref, split_ref, sums_ref
 ):
     split_tiles(tiles_ref, split_ref, 0, CAP)
     far, near = places()
-    slot = slot_of(far, FAR_ORDER)
+    slot = far_slot(far)
     lines = -(-LINE // TB)
     index = [
         [in_ref[i, MSG * k + CAP : MSG * (k + 1), :] for k in range(lines)] for i in range(NEAR)
@@ -241,7 +248,9 @@
     for i in range(NEAR):
         gradient += picked_sum(hits_of(own_wanted, index[i], LINE), in_ref[i])
     gradient_ref[...] = gradient
-    send_forward(gradient[:CAP], split_ref, info_ref, info_ref[2 * CAP : 2 * CAP + 1, :], out_ref)
+    sums = forward(gradient, split_ref, info_ref)
+    sums_ref[...] = sums
+    send_to_all(out_ref, COLS, sums, info_ref[2 * CAP : 2 * CAP + 1, :])
 
 
 def send_backward(picked, split_ref, info_ref, scalars, out_ref):
@@ -279,17 +288,22 @@
 
 
 def second_gradient_kernel(
-    info_ref, in_ref, split_ref, gradient_ref, out_ref, product_ref, next_ref, state_ref
+    info_ref, in_ref, split_ref, gradient_ref, sums_ref,
+    out_ref, product_ref, next_ref, state_ref, product_sums_ref, next_sums_ref,
 ):
     total = added(in_ref)
     product = total[:WANT]
+    product_sums = forward(product, split_ref, info_ref)
+    product_sums_ref[...] = product_sums
     norm, image_norm = scalars_of(total[WANT : WANT + 1], 2)
     step = norm / image_norm
     following = gradient_ref[...] - step * product
     product_ref[...] = product
     next_ref[...] = following
     state_ref[...] = stack_rows([norm, image_norm, step])
-    send_forward(following[:CAP], split_ref, info_ref, jnp.zeros((1, TB), F32), out_ref)
+    next_sums = sums_ref[...] - step * product_sums
+    next_sums_ref[...] = next_sums
+    send_to_all(out_ref, COLS, next_sums, jnp.zeros((1, TB), F32))
 
 
 def second_image_kernel(
@@ -306,9 +320,10 @@
 
 def third_gradient_kernel(
     info_ref, in_ref, split_ref, first_ref, second_ref, product_ref, state_ref,
-    out_ref, keep_ref, later_ref,
+    product_sums_ref, second_sums_ref, out_ref, keep_ref, later_ref,
 ):
     total = added(in_ref)
+    product_sums = forward(total, split_ref, info_ref)
     old_norm, old_image_norm, old_step = state_ref[0:1, :], state_ref[1:2, :], state_ref[2:3, :]
     norm, straight, cross = scalars_of(total[WANT : WANT + 1], 3)
     ratio = norm / old_norm
@@ -323,7 +338,8 @@
     keep_ref[1] = direction[CAP:]
     keep_ref[2] = weights[CAP:]
     later_ref[...] = stack_rows([norm, image_norm, step, ratio])
-    send_forward(third[:CAP], split_ref, info_ref, jnp.zeros((1, TB), F32), out_ref)
+    product_sums = product_sums + ratio * product_sums_ref[...]
+    send_to_all(out_ref, COLS, second_sums_ref[...] - step * product_sums, jnp.zeros((1, TB), F32))
 
 
 def third_image_kernel(
@@ -367,9 +383,13 @@
 
 
 GROUPS = {
-    "far": [[far * NEAR + near for far in FAR_ORDER] for near in range(NEAR)],
+    "far": [
+        [(far * NEAR + near) * COLS + col for far in FAR_ORDERS[col % 2]]
+        for near in range(NEAR)
+        for col in range(COLS)
+    ],
     "near": [[far * NEAR + near for near in NEAR_ORDER] for far in range(FAR)],
-    "rows": [[far * NEAR + near for far in FAR_ORDER for near in NEAR_ORDER]],
+    "rows": [[far * NEAR + near for far in FAR_ORDERS[0] for near in NEAR_ORDER]],
     "cols": [COL_ORDER],
 }
 
@@ -378,7 +398,8 @@
     shape = x.shape
     if len(shape) == 2:
         x = x.reshape(count, shape[0] // count, 1, TB)
-    axis, groups = "cols" if kind == "cols" else "rows", GROUPS[kind]
+    axis = {"cols": "cols", "far": ("rows", "cols")}.get(kind, "rows")
+    groups = GROUPS[kind]
     return lax.all_to_all(x, axis, 0, 0, axis_index_groups=groups, tiled=True).reshape(shape)
 
 
@@ -387,6 +408,7 @@
     b = lambda *shape: (shape, BF16)
     to_far, to_near = f(LINE, TB), f(NEAR * HAND, TB)
     to_cols = f(SIDE, TB)
+    own = f(CAP, TB)
     image_shape, state_shape = f(ROW_BLOCKS, TB), f(EXTRA, TB)
 
     message, info = call(
@@ -407,9 +429,9 @@
         62 * 2**20,
     )
     (message,) = call(relay_kernel, [f(NEAR, LINE, TB)], [swap(message, "far", FAR)])
-    message, first, hand_hits, split = call(
+    message, first, hand_hits, split, first_sums = call(
         gathered_kernel,
-        [to_cols, f(WANT, TB), b(NEAR * WANT, LINE), b(CAP, 2 * TB, TB)],
+        [to_cols, f(WANT, TB), b(NEAR * WANT, LINE), b(CAP, 2 * TB, TB), own],
         [info, swap(message, "near", NEAR), tiles],
     )
     message, image, row_hits = call(
@@ -418,10 +440,10 @@
         [info, swap(message, "cols", COLS), split, scores],
     )
     (message,) = call(hand_kernel, [to_near], [swap(message, "far", FAR), hand_hits])
-    message, product, second, state = call(
+    message, product, second, state, product_sums, second_sums = call(
         second_gradient_kernel,
-        [to_cols, f(WANT, TB), f(WANT, TB), state_shape],
-        [info, swap(message, "near", NEAR), split, first],
+        [to_cols, f(WANT, TB), f(WANT, TB), state_shape, own, own],
+        [info, swap(message, "near", NEAR), split, first, first_sums],
     )
     message, second_image = call(
         second_image_kernel,
@@ -432,7 +454,10 @@
     message, keep, later = call(
         third_gradient_kernel,
         [to_cols, f(3, SHARE, TB), state_shape],
-        [info, swap(message, "near", NEAR), split, first, second, product, state],
+        [
+            info, swap(message, "near", NEAR), split, first, second, product, state,
+            product_sums, second_sums,
+        ],
     )
     message, images = call(
         third_image_kernel,

time: 142 us -> 141 us (level)
  no operation moved by 1% of the time
where the time goes in v8:
time: 141 us; the launch traced here: 140 us
  blocking collectives  132 us (94%)
  Pallas kernels  7.17 us (5%)
    all_to_all x10, blocking collectives, swap(): lax.all_to_all(x, axis, 0, 0, axis_index_groups=groups, tiled=True)  132 us
    pallas_call x11, Pallas kernels, call(): pl.pallas_call(kernel, out_shape=[jax.ShapeDtypeStruct(s, d) for s, d in...  7.17 us

profile of v8, /device:TPU:1, one launch (start us, length us, event | category | flops | bytes accessed | tf_op | source)
XLA Modules:
  0.0 140.2 jit_solution(13000180863331903061)
XLA Ops:
  1.3 2.5 %first_kernel.1 = (f32[200,128]{1,0:T(8,128)}, f32[56,128]{1,0:T(8,128)}) custom-call(s32[24]{0:T(128)} %row_hbm.1, s32[24]{0:T(128)} %col_hbm.1, s32[1]{0:T(128)S(6)} %copy.16.live_hbm, f32[24,128,128]{2,1,0:T(8,128)} %tiles_ref.1, f32[256,128]{1,0:T(8,128)} %scores_ref.5), custom_call_target="tpu_custom_call" | custom-call | tf_op jit(solution)/shard_map/first_kernel/pallas_call | solution.py:374
  3.8 0.0 copy-start
  3.8 0.0 copy-start.2
  3.8 21.9 %all_to_all.50 = f32[8,25,1,128]{3,2,1,0:T(1,128)S(1)} all-to-all(f32[8,25,1,128]{3,2,1,0:T(1,128)} %bitcast.37), channel_id=1, replica_groups={{256,0,64,448,128,384,192,320},{257,1,449,65,385,129,321,193},{258,2,66..., dimensions={0} | all-to-all | bytes 204800 | tf_op jit(solution)/shard_map/all_to_all | solution.py:403
  25.7 0.1 relay_kernel.1
  25.8 15.0 %all_to_all.51.in_ref = f32[8,200,128]{2,1,0:T(8,128)S(1)} all-to-all(f32[8,200,128]{2,1,0:T(8,128)S(1)} %relay_kernel.1), channel_id=1, replica_groups={{16,24,32,40,48,56,0,8},{80,88,96,104,112,120,64,72},{144,152,160,168,1..., dimensions={0} | all-to-all | bytes 1638400 | tf_op jit(solution)/shard_map/all_to_all | solution.py:403
  40.8 0.0 copy-start.1
  40.8 0.0 copy-done
  40.8 0.0 copy-done.2
  40.8 0.9 gathered_kernel.1
  41.8 10.7 %all_to_all.52 = f32[8,25,1,128]{3,2,1,0:T(1,128)S(1)} all-to-all(f32[8,25,1,128]{3,2,1,0:T(1,128)S(1)} %bitcast.33), channel_id=1, replica_groups={{5,1,7,3,4,0,6,2},{13,9,15,11,12,8,14,10},{21,17,23,19,20,16,22,18},{29..., dimensions={0} | all-to-all | bytes 204800 | tf_op jit(solution)/shard_map/all_to_all | solution.py:403
  52.4 0.0 copy-done.1
  52.4 0.6 first_image_kernel.1
  53.1 16.9 %all_to_all.53 = f32[8,25,1,128]{3,2,1,0:T(1,128)S(1)} all-to-all(f32[8,25,1,128]{3,2,1,0:T(1,128)S(1)} %bitcast.34), channel_id=1, replica_groups={{256,0,64,448,128,384,192,320},{257,1,449,65,385,129,321,193},{258,2,66..., dimensions={0} | all-to-all | bytes 204800 | tf_op jit(solution)/shard_map/all_to_all | solution.py:403
  69.9 0.2 hand_kernel.2
  70.1 8.8 %all_to_all.54 = f32[8,41,1,128]{3,2,1,0:T(1,128)S(1)} all-to-all(f32[8,41,1,128]{3,2,1,0:T(1,128)S(1)} %bitcast.23), channel_id=1, replica_groups={{16,24,32,40,48,56,0,8},{80,88,96,104,112,120,64,72},{144,152,160,168,1..., dimensions={0} | all-to-all | bytes 335872 | tf_op jit(solution)/shard_map/all_to_all | solution.py:403
  78.9 0.5 second_gradient_kernel.1
  79.5 8.5 %all_to_all.55 = f32[8,25,1,128]{3,2,1,0:T(1,128)S(1)} all-to-all(f32[8,25,1,128]{3,2,1,0:T(1,128)S(1)} %bitcast.32), channel_id=1, replica_groups={{5,1,7,3,4,0,6,2},{13,9,15,11,12,8,14,10},{21,17,23,19,20,16,22,18},{29..., dimensions={0} | all-to-all | bytes 204800 | tf_op jit(solution)/shard_map/all_to_all | solution.py:403
  88.0 0.6 second_image_kernel.1
  88.6 16.5 %all_to_all.56 = f32[8,25,1,128]{3,2,1,0:T(1,128)S(1)} all-to-all(f32[8,25,1,128]{3,2,1,0:T(1,128)S(1)} %bitcast.35), channel_id=1, replica_groups={{256,0,64,448,128,384,192,320},{257,1,449,65,385,129,321,193},{258,2,66..., dimensions={0} | all-to-all | bytes 204800 | tf_op jit(solution)/shard_map/all_to_all | solution.py:403
  105.0 0.2 hand_kernel.3
  105.2 8.4 %all_to_all.57 = f32[8,41,1,128]{3,2,1,0:T(1,128)S(1)} all-to-all(f32[8,41,1,128]{3,2,1,0:T(1,128)S(1)} %bitcast.22), channel_id=1, replica_groups={{16,24,32,40,48,56,0,8},{80,88,96,104,112,120,64,72},{144,152,160,168,1..., dimensions={0} | all-to-all | bytes 335872 | tf_op jit(solution)/shard_map/all_to_all | solution.py:403
  113.6 0.5 third_gradient_kernel.1
  114.1 8.5 %all_to_all.58 = f32[8,25,1,128]{3,2,1,0:T(1,128)S(1)} all-to-all(f32[8,25,1,128]{3,2,1,0:T(1,128)S(1)} %bitcast.31), channel_id=1, replica_groups={{5,1,7,3,4,0,6,2},{13,9,15,11,12,8,14,10},{21,17,23,19,20,16,22,18},{29..., dimensions={0} | all-to-all | bytes 204800 | tf_op jit(solution)/shard_map/all_to_all | solution.py:403
  122.6 0.3 third_image_kernel.1
  122.9 16.5 %all_to_all.59 = f32[64,1,1,128]{3,2,1,0:T(1,128)S(1)} all-to-all(f32[64,1,1,128]{3,2,1,0:T(1,128)S(1)} %bitcast.36), channel_id=1, replica_groups={{272,280,288,296,304,312,256,264,16,24,32,40,48,56,0,8,80,88,96,104,112..., dimensions={0} | all-to-all | bytes 65536 | tf_op jit(solution)/shard_map/all_to_all | solution.py:403
  139.4 0.8 last_kernel.1
Async XLA Ops:
  3.8 37.0 %copy-start = (f32[24,128,128]{2,1,0:T(8,128)S(1)}, f32[24,128,128]{2,1,0:T(8,128)}, u32[]{:S(2)}) copy-start(f32[24,128,128]{2,1,0:T(8,128)} %tiles_ref.1) | copy-start | bytes 4718596
  3.8 37.0 %copy-start.2 = (f32[56,128]{1,0:T(8,128)S(1)}, f32[56,128]{1,0:T(8,128)}, u32[]{:S(2)}) copy-start(f32[56,128]{1,0:T(8,128)} %get-tuple-element.25.info_ref) | copy-start | bytes 86020
  40.8 11.6 %copy-start.1 = (f32[256,128]{1,0:T(8,128)S(1)}, f32[256,128]{1,0:T(8,128)}, u32[]{:S(2)}) copy-start(f32[256,128]{1,0:T(8,128)} %scores_ref.5) | copy-start | bytes 393220

commit v9 on v8

--- a/solution.py
+++ b/solution.py
@@ -396,7 +396,9 @@
 
 def swap(x, kind, count):
     shape = x.shape
-    if len(shape) == 2:
+    if shape == (count, TB):
+        x = x.reshape(count * TB)
+    elif len(shape) == 2:
         x = x.reshape(count, shape[0] // count, 1, TB)
     axis = {"cols": "cols", "far": ("rows", "cols")}.get(kind, "rows")
     groups = GROUPS[kind]

time: 141 us -> 141 us (level)
  no operation moved by 1% of the time
where the time goes in v9:
time: 141 us; the launch traced here: 140 us
  blocking collectives  132 us (94%)
  Pallas kernels  7.17 us (5%)
    all_to_all x10, blocking collectives, swap(): lax.all_to_all(x, axis, 0, 0, axis_index_groups=groups, tiled=True)  132 us
    pallas_call x11, Pallas kernels, call(): pl.pallas_call(kernel, out_shape=[jax.ShapeDtypeStruct(s, d) for s, d in...  7.17 us

profile of v9, /device:TPU:1, one launch (start us, length us, event | category | flops | bytes accessed | tf_op | source)
XLA Modules:
  0.0 140.2 jit_solution(13000180863331903061)
XLA Ops:
  1.3 2.5 %first_kernel.1 = (f32[200,128]{1,0:T(8,128)}, f32[56,128]{1,0:T(8,128)}) custom-call(s32[24]{0:T(128)} %row_hbm.1, s32[24]{0:T(128)} %col_hbm.1, s32[1]{0:T(128)S(6)} %copy.16.live_hbm, f32[24,128,128]{2,1,0:T(8,128)} %tiles_ref.1, f32[256,128]{1,0:T(8,128)} %scores_ref.5), custom_call_target="tpu_custom_call" | custom-call | tf_op jit(solution)/shard_map/first_kernel/pallas_call | solution.py:374
  3.8 0.0 copy-start
  3.8 0.0 copy-start.2
  3.8 21.9 %all_to_all.54 = f32[8,25,1,128]{3,2,1,0:T(1,128)S(1)} all-to-all(f32[8,25,1,128]{3,2,1,0:T(1,128)} %bitcast.37), channel_id=1, replica_groups={{256,0,64,448,128,384,192,320},{257,1,449,65,385,129,321,193},{258,2,66..., dimensions={0} | all-to-all | bytes 204800 | tf_op jit(solution)/shard_map/all_to_all | solution.py:405
  25.7 0.1 relay_kernel.1
  25.8 15.0 %all_to_all.55.in_ref = f32[8,200,128]{2,1,0:T(8,128)S(1)} all-to-all(f32[8,200,128]{2,1,0:T(8,128)S(1)} %relay_kernel.1), channel_id=1, replica_groups={{16,24,32,40,48,56,0,8},{80,88,96,104,112,120,64,72},{144,152,160,168,1..., dimensions={0} | all-to-all | bytes 1638400 | tf_op jit(solution)/shard_map/all_to_all | solution.py:405
  40.8 0.0 copy-start.1
  40.8 0.0 copy-done
  40.8 0.0 copy-done.2
  40.8 0.9 gathered_kernel.1
  41.8 10.7 %all_to_all.56 = f32[8,25,1,128]{3,2,1,0:T(1,128)S(1)} all-to-all(f32[8,25,1,128]{3,2,1,0:T(1,128)S(1)} %bitcast.33), channel_id=1, replica_groups={{5,1,7,3,4,0,6,2},{13,9,15,11,12,8,14,10},{21,17,23,19,20,16,22,18},{29..., dimensions={0} | all-to-all | bytes 204800 | tf_op jit(solution)/shard_map/all_to_all | solution.py:405
  52.4 0.0 copy-done.1
  52.4 0.6 first_image_kernel.1
  53.1 16.9 %all_to_all.57 = f32[8,25,1,128]{3,2,1,0:T(1,128)S(1)} all-to-all(f32[8,25,1,128]{3,2,1,0:T(1,128)S(1)} %bitcast.34), channel_id=1, replica_groups={{256,0,64,448,128,384,192,320},{257,1,449,65,385,129,321,193},{258,2,66..., dimensions={0} | all-to-all | bytes 204800 | tf_op jit(solution)/shard_map/all_to_all | solution.py:405
  69.9 0.2 hand_kernel.2
  70.1 8.8 %all_to_all.58 = f32[8,41,1,128]{3,2,1,0:T(1,128)S(1)} all-to-all(f32[8,41,1,128]{3,2,1,0:T(1,128)S(1)} %bitcast.23), channel_id=1, replica_groups={{16,24,32,40,48,56,0,8},{80,88,96,104,112,120,64,72},{144,152,160,168,1..., dimensions={0} | all-to-all | bytes 335872 | tf_op jit(solution)/shard_map/all_to_all | solution.py:405
  78.9 0.5 second_gradient_kernel.1
  79.5 8.5 %all_to_all.59 = f32[8,25,1,128]{3,2,1,0:T(1,128)S(1)} all-to-all(f32[8,25,1,128]{3,2,1,0:T(1,128)S(1)} %bitcast.32), channel_id=1, replica_groups={{5,1,7,3,4,0,6,2},{13,9,15,11,12,8,14,10},{21,17,23,19,20,16,22,18},{29..., dimensions={0} | all-to-all | bytes 204800 | tf_op jit(solution)/shard_map/all_to_all | solution.py:405
  88.0 0.6 second_image_kernel.1
  88.6 16.5 %all_to_all.60 = f32[8,25,1,128]{3,2,1,0:T(1,128)S(1)} all-to-all(f32[8,25,1,128]{3,2,1,0:T(1,128)S(1)} %bitcast.35), channel_id=1, replica_groups={{256,0,64,448,128,384,192,320},{257,1,449,65,385,129,321,193},{258,2,66..., dimensions={0} | all-to-all | bytes 204800 | tf_op jit(solution)/shard_map/all_to_all | solution.py:405
  105.0 0.2 hand_kernel.3
  105.2 8.4 %all_to_all.61 = f32[8,41,1,128]{3,2,1,0:T(1,128)S(1)} all-to-all(f32[8,41,1,128]{3,2,1,0:T(1,128)S(1)} %bitcast.22), channel_id=1, replica_groups={{16,24,32,40,48,56,0,8},{80,88,96,104,112,120,64,72},{144,152,160,168,1..., dimensions={0} | all-to-all | bytes 335872 | tf_op jit(solution)/shard_map/all_to_all | solution.py:405
  113.6 0.5 third_gradient_kernel.1
  114.1 8.5 %all_to_all.62 = f32[8,25,1,128]{3,2,1,0:T(1,128)S(1)} all-to-all(f32[8,25,1,128]{3,2,1,0:T(1,128)S(1)} %bitcast.31), channel_id=1, replica_groups={{5,1,7,3,4,0,6,2},{13,9,15,11,12,8,14,10},{21,17,23,19,20,16,22,18},{29..., dimensions={0} | all-to-all | bytes 204800 | tf_op jit(solution)/shard_map/all_to_all | solution.py:405
  122.6 0.3 third_image_kernel.1
  122.9 16.5 %all_to_all.63 = f32[64,128,1]{1,2,0:T(1,128)S(1)} all-to-all(f32[64,128,1]{1,2,0:T(1,128)S(1)} %bitcast.36), channel_id=1, replica_groups={{272,280,288,296,304,312,256,264,16,24,32,40,48,56,0,8,80,88,96,104,112..., dimensions={0} | all-to-all | bytes 65536 | tf_op jit(solution)/shard_map/all_to_all | solution.py:405
  139.4 0.8 last_kernel.1
Async XLA Ops:
  3.8 37.0 %copy-start = (f32[24,128,128]{2,1,0:T(8,128)S(1)}, f32[24,128,128]{2,1,0:T(8,128)}, u32[]{:S(2)}) copy-start(f32[24,128,128]{2,1,0:T(8,128)} %tiles_ref.1) | copy-start | bytes 4718596
  3.8 37.0 %copy-start.2 = (f32[56,128]{1,0:T(8,128)S(1)}, f32[56,128]{1,0:T(8,128)}, u32[]{:S(2)}) copy-start(f32[56,128]{1,0:T(8,128)} %get-tuple-element.25.info_ref) | copy-start | bytes 86020
  40.8 11.6 %copy-start.1 = (f32[256,128]{1,0:T(8,128)S(1)}, f32[256,128]{1,0:T(8,128)}, u32[]{:S(2)}) copy-start(f32[256,128]{1,0:T(8,128)} %scores_ref.5) | copy-start | bytes 393220
